TPU v7x, 768 devices: a whole 4x8x12 slice. The times are simulated.
768 devices in a mesh: sub: 32 (over y, x), col: 24 (over z, core).
Axes of the slice: x: 4, y: 8, z: 12, core: 2. Of those that a mesh axis runs over, the one named last changes fastest.
Arguments:
- inv_conductance: bfloat16 [2, 2048, 2048], P(None, 'sub'), may hold values from -1 to 1
- source: bfloat16 [96, 2, 2048], P('col', None, 'sub'), may hold values from -6 to 6
- line_ends: int32 [64, 2], replicated, may hold values from 0 to 4095, as said below
- delays: int32 [64], replicated, may hold values from 2 to 6
- admittance: float32 [64], replicated, may hold values from 0.3 to 1.2
- breaker: int32 [64, 96], P(None, 'col'), may hold values 0 or 1
- hist_volt: float32 [6, 96, 128], P(None, 'col'), may hold values from -4 to 4
- hist_inj: float32 [6, 96, 128], P(None, 'col'), may hold values from -4 to 4
- station_node: int32 [48], replicated, may hold values from 0 to 4095
- station_initial: float32 [96, 48], P(None, 'col'), may hold values from -4 to 4
- capacitor_initial: float32 [96, 48, 2400], P(None, 'col', 'sub'), may hold values from 0.6 to 1.4
- insert_count: int32 [8, 96, 48], P(None, None, 'col'), may hold values from 600 to 1800
Outputs:
- node_voltages: float32 [96, 2, 2048], P('col', None, 'sub')
- capacitor_volts: float32 [96, 48, 2400], P(None, 'col', 'sub')
- station_current: float32 [8, 96, 48], P(None, None, 'col')
Inputs may be any that keep to these rules, and one draw needn't show every extreme that they name: `line_ends`: each line joins a node of one subnetwork to a node of another.
All inputs are finite; a program needn't handle non-finite values. No bound on the sum of `breaker` on one device may be relied on, other than what follows from the above.
Results may differ from a plain program's by a relative error of at most 0.0014.
Values may be sent and summed in bfloat16 or wider, within the bound.
A program may use at most 32 MiB of HBM per device.

v0:
```python
import jax
import jax.numpy as jnp
from jax import lax
from jax.sharding import PartitionSpec as P

SM = 2400
STEPS = 8
DMIN = 2
DMAX = 6


charge_rate = 0.5


def swap_ends(values):
    full_shape = values.shape
    paired = values.reshape(full_shape[:-1] + (full_shape[-1] // 2, 2))
    return paired[..., ::-1].reshape(full_shape)


def local_slots(node_ids, node_count, row_count, sub_index):
    sub_id = node_ids // node_count
    node_local = node_ids % node_count
    is_mine = node_local // row_count == sub_index
    slot_index = jnp.where(is_mine, sub_id * row_count + node_local - sub_index * row_count, 0)
    return (slot_index, is_mine)


def per_device(
    inv_conductance,
    source,
    line_ends,
    delays,
    admittance,
    breaker,
    hist_volt,
    hist_inj,
    station_node,
    station_initial,
    capacitor_initial,
    insert_count,
):
    sub_count, row_count, node_count = inv_conductance.shape
    col_count = source.shape[0]
    sub_index = lax.axis_index("sub")
    end_nodes = line_ends.reshape(-1)
    end_total = end_nodes.shape[0]
    end_delay = jnp.repeat(delays, 2)
    end_admit = jnp.repeat(admittance, 2)
    end_mask = jnp.repeat(breaker, 2, axis=0).T.astype(jnp.float32)
    end_slot, end_owned = local_slots(end_nodes, node_count, row_count, sub_index)
    station_slot, station_owned = local_slots(station_node, node_count, row_count, sub_index)
    volt_buffer = (
        jnp.zeros((DMAX + STEPS, col_count, end_total), jnp.float32).at[:DMAX].set(hist_volt)
    )
    inj_buffer = (
        jnp.zeros((DMAX + STEPS, col_count, end_total), jnp.float32).at[:DMAX].set(hist_inj)
    )
    module_count = capacitor_initial.shape[2]
    position = sub_index * module_count + jnp.arange(module_count, dtype=jnp.int32)
    source_part = jnp.einsum(
        "srk,csk->csr",
        inv_conductance,
        lax.all_gather(source, "sub", axis=2, tiled=True),
        preferred_element_type=jnp.float32,
    )
    capacitor = capacitor_initial
    node_part = jnp.zeros_like(station_initial)
    currents = []
    voltages = jnp.zeros((col_count, sub_count, row_count), jnp.float32)
    for step_index in range(STEPS):
        read_index = step_index + DMAX - end_delay
        selector = jnp.broadcast_to(read_index[None, None, :], (1, col_count, end_total))
        volt_read = jnp.take_along_axis(volt_buffer, selector, axis=0)[0]
        inj_read = jnp.take_along_axis(inj_buffer, selector, axis=0)[0]
        injection = end_mask * (2.0 * end_admit * swap_ends(volt_read) - swap_ends(inj_read))
        inj_buffer = inj_buffer.at[DMAX + step_index].set(injection)
        inserted_count = insert_count[step_index]
        inserted = (position < inserted_count[..., None]).astype(jnp.float32)
        thevenin_part = 2.0 / SM * jnp.sum(inserted * capacitor, axis=-1)
        thevenin, node_volt = lax.psum((thevenin_part, node_part), "sub")
        if step_index == 0:
            node_volt = node_volt + station_initial
        current = (thevenin - node_volt) / (1.0 + inserted_count.astype(jnp.float32) / SM)
        capacitor = capacitor - charge_rate * inserted * current[..., None]
        currents.append(current)
        current_col = lax.all_to_all(current, "col", split_axis=0, concat_axis=1, tiled=True)
        term_full = jnp.zeros((col_count, sub_count * node_count), jnp.float32)
        term_full = term_full.at[:, end_nodes].add(injection).at[:, station_node].add(current_col)
        term_full = term_full.astype(jnp.bfloat16).reshape(col_count, sub_count, node_count)
        voltages = source_part + jnp.einsum(
            "srk,csk->csr", inv_conductance, term_full, preferred_element_type=jnp.float32
        )
        flat_volts = voltages.reshape(col_count, sub_count * row_count)
        end_part = jnp.where(end_owned, flat_volts[:, end_slot], 0.0)
        if step_index + 1 < STEPS:
            station_part = jnp.where(station_owned, flat_volts[:, station_slot], 0.0)
            node_part = lax.all_to_all(station_part, "col", split_axis=1, concat_axis=0, tiled=True)
        if step_index + DMIN < STEPS:
            volt_buffer = volt_buffer.at[DMAX + step_index].set(lax.psum(end_part, "sub"))
    return (voltages, capacitor, jnp.stack(currents))


def solution(mesh):
    in_specs = (
        P(None, "sub", None),
        P("col", None, "sub"),
        P(),
        P(),
        P(),
        P(None, "col"),
        P(None, "col", None),
        P(None, "col", None),
        P(),
        P(None, "col"),
        P(None, "col", "sub"),
        P(None, None, "col"),
    )
    out_specs = (P("col", None, "sub"), P(None, "col", "sub"), P(None, None, "col"))
    return jax.shard_map(
        per_device, mesh=mesh, in_specs=in_specs, out_specs=out_specs, check_vma=False
    )
```

profile of v0, /device:TPU:1, one launch (start us, length us, event | category | flops | bytes accessed | tf_op | source)
XLA Modules:
  0.0 954.9 jit_solution(14284137142761814809)
XLA Ops:
  2.6 61.9 %psum.150 = f32[96,2]{0,1:T(2,128)S(1)} all-reduce(f32[96,2]{0,1:T(2,128)S(1)} %broadcast_multiply_fusion.7), channel_id=1, replica_groups=mesh['sub'=32,'col'=24] {'sub'}, use_global_device_ids=true, to_apply=%region_2.4 | all-reduce | flops 192 | bytes 1536 | tf_op jit(solution)/shard_map/psum | solution.py:81
  65.9 30.1 %all-to-all-start = ((f32[24,4,2]{1,2,0:T(2,128)}), f32[24,4,2]{1,2,0:T(2,128)S(1)}, u32[]{:S(2)}, u32[]{:S(2)}) async-start(f32[24,4,2]{1,2,0:T(2,128)} %copy.235), calls=%async_computation | async-start | bytes 49152 | tf_op jit(solution)/shard_map/all_to_all | solution.py:87
  112.4 34.8 %all_gather.3 = bf16[4,2,2048]{0,1,2:T(2,128)(2,1)S(1)} all-gather(bf16[4,2,64]{0,1,2:T(2,128)(2,1)S(1)} %copy.224), channel_id=1, replica_groups=mesh['sub'=32,'col'=24] {'sub'}, dimensions={2}, use_global_device_ids=true | all-gather | bytes 33792 | tf_op jit(solution)/shard_map/all_gather | solution.py:64
  158.4 21.9 %all-to-all-start.1 = ((f32[4,24,2]{0,2,1:T(2,128)}), f32[4,24,2]{0,2,1:T(2,128)S(1)}, u32[]{:S(2)}, u32[]{:S(2)}) async-start(f32[4,24,2]{0,2,1:T(2,128)} %broadcast_select_fusion.6), calls=%async_computation.1 | async-start | bytes 49152 | tf_op jit(solution)/shard_map/all_to_all | solution.py:98
  181.0 9.1 all-to-all-done.1
  190.2 58.1 %all-reduce.8 = (f32[1,4,128]{2,1,0:T(4,128)S(1)}, f32[96,2]{0,1:T(2,128)S(1)}, f32[96,2]{0,1:T(2,128)S(1)}) all-reduce(f32[1,4,128]{2,1,0:T(4,128)S(1)} %select_bitcast_fusion.13, f32[96,2]{0,1:T(2,128)S(1)} %broadcast_multiply_fusion.6, f32[96,2]{0,1:T(2,128)S(1)} %all_to_all.202), channel_id=1, replica_groups=mesh['sub'=32,'col'=24] {'sub'}, use_global_device_ids=true, to_apply=%region_4.6 | all-reduce | flops 896 | bytes 7168 | tf_op jit(solution)/shard_map/psum | solution.py:100
  249.0 18.1 %all-to-all-start.2 = ((f32[24,4,2]{1,2,0:T(2,128)}), f32[24,4,2]{1,2,0:T(2,128)S(1)}, u32[]{:S(2)}, u32[]{:S(2)}) async-start(f32[24,4,2]{1,2,0:T(2,128)} %copy.247), calls=%async_computation.2 | async-start | bytes 49152 | tf_op jit(solution)/shard_map/all_to_all | solution.py:87
  283.8 9.8 %all-to-all-start.3 = ((f32[4,24,2]{0,2,1:T(2,128)}), f32[4,24,2]{0,2,1:T(2,128)S(1)}, u32[]{:S(2)}, u32[]{:S(2)}) async-start(f32[4,24,2]{0,2,1:T(2,128)} %broadcast_select_fusion.5), calls=%async_computation.3 | async-start | bytes 49152 | tf_op jit(solution)/shard_map/all_to_all | solution.py:98
  293.6 9.7 %all-to-all-done.3 = f32[4,24,2]{0,2,1:T(2,128)S(1)} async-done(((f32[4,24,2]{0,2,1:T(2,128)}), f32[4,24,2]{0,2,1:T(2,128)S(1)}, u32[]{:S(2)}, u32[]{:S(2)}) %all-to-all-start.3) | async-done | bytes 800 | tf_op jit(solution)/shard_map/all_to_all | solution.py:98
  303.4 56.1 %all-reduce.7 = (f32[1,4,128]{2,1,0:T(4,128)S(1)}, f32[96,2]{0,1:T(2,128)S(1)}, f32[96,2]{0,1:T(2,128)S(1)}) all-reduce(f32[1,4,128]{2,1,0:T(4,128)S(1)} %select_bitcast_fusion.12, f32[96,2]{0,1:T(2,128)S(1)} %broadcast_multiply_fusion.5, f32[96,2]{0,1:T(2,128)S(1)} %all_to_all.209), channel_id=1, replica_groups=mesh['sub'=32,'col'=24] {'sub'}, use_global_device_ids=true, to_apply=%region_10.12 | all-reduce | flops 896 | bytes 7168 | tf_op jit(solution)/shard_map/psum | solution.py:100
  360.2 17.5 %all-to-all-start.4 = ((f32[24,4,2]{1,2,0:T(2,128)}), f32[24,4,2]{1,2,0:T(2,128)S(1)}, u32[]{:S(2)}, u32[]{:S(2)}) async-start(f32[24,4,2]{1,2,0:T(2,128)} %copy.259), calls=%async_computation.4 | async-start | bytes 49152 | tf_op jit(solution)/shard_map/all_to_all | solution.py:87
  394.4 9.8 %all-to-all-start.5 = ((f32[4,24,2]{0,2,1:T(2,128)}), f32[4,24,2]{0,2,1:T(2,128)S(1)}, u32[]{:S(2)}, u32[]{:S(2)}) async-start(f32[4,24,2]{0,2,1:T(2,128)} %broadcast_select_fusion.4), calls=%async_computation.5 | async-start | bytes 49152 | tf_op jit(solution)/shard_map/all_to_all | solution.py:98
  404.2 9.7 %all-to-all-done.5 = f32[4,24,2]{0,2,1:T(2,128)S(1)} async-done(((f32[4,24,2]{0,2,1:T(2,128)}), f32[4,24,2]{0,2,1:T(2,128)S(1)}, u32[]{:S(2)}, u32[]{:S(2)}) %all-to-all-start.5) | async-done | bytes 800 | tf_op jit(solution)/shard_map/all_to_all | solution.py:98
  414.0 57.9 %all-reduce.6 = (f32[1,4,128]{2,1,0:T(4,128)S(1)}, f32[96,2]{0,1:T(2,128)S(1)}, f32[96,2]{0,1:T(2,128)S(1)}) all-reduce(f32[1,4,128]{2,1,0:T(4,128)S(1)} %select_bitcast_fusion.11, f32[96,2]{0,1:T(2,128)S(1)} %broadcast_multiply_fusion.4, f32[96,2]{0,1:T(2,128)S(1)} %all_to_all.216), channel_id=1, replica_groups=mesh['sub'=32,'col'=24] {'sub'}, use_global_device_ids=true, to_apply=%region_16.18 | all-reduce | flops 896 | bytes 7168 | tf_op jit(solution)/shard_map/psum | solution.py:100
  472.7 17.6 %all-to-all-start.6 = ((f32[24,4,2]{1,2,0:T(2,128)}), f32[24,4,2]{1,2,0:T(2,128)S(1)}, u32[]{:S(2)}, u32[]{:S(2)}) async-start(f32[24,4,2]{1,2,0:T(2,128)} %copy.271), calls=%async_computation.6 | async-start | bytes 49152 | tf_op jit(solution)/shard_map/all_to_all | solution.py:87
  507.0 9.8 %all-to-all-start.7 = ((f32[4,24,2]{0,2,1:T(2,128)}), f32[4,24,2]{0,2,1:T(2,128)S(1)}, u32[]{:S(2)}, u32[]{:S(2)}) async-start(f32[4,24,2]{0,2,1:T(2,128)} %broadcast_select_fusion.3), calls=%async_computation.7 | async-start | bytes 49152 | tf_op jit(solution)/shard_map/all_to_all | solution.py:98
  516.8 9.7 %all-to-all-done.7 = f32[4,24,2]{0,2,1:T(2,128)S(1)} async-done(((f32[4,24,2]{0,2,1:T(2,128)}), f32[4,24,2]{0,2,1:T(2,128)S(1)}, u32[]{:S(2)}, u32[]{:S(2)}) %all-to-all-start.7) | async-done | bytes 800 | tf_op jit(solution)/shard_map/all_to_all | solution.py:98
  526.6 56.1 %all-reduce.5 = (f32[1,4,128]{2,1,0:T(4,128)S(1)}, f32[96,2]{0,1:T(2,128)S(1)}, f32[96,2]{0,1:T(2,128)S(1)}) all-reduce(f32[1,4,128]{2,1,0:T(4,128)S(1)} %select_bitcast_fusion.10, f32[96,2]{0,1:T(2,128)S(1)} %broadcast_multiply_fusion.3, f32[96,2]{0,1:T(2,128)S(1)} %all_to_all.223), channel_id=1, replica_groups=mesh['sub'=32,'col'=24] {'sub'}, use_global_device_ids=true, to_apply=%region_22.24 | all-reduce | flops 896 | bytes 7168 | tf_op jit(solution)/shard_map/psum | solution.py:100
  583.4 17.5 %all-to-all-start.8 = ((f32[24,4,2]{1,2,0:T(2,128)}), f32[24,4,2]{1,2,0:T(2,128)S(1)}, u32[]{:S(2)}, u32[]{:S(2)}) async-start(f32[24,4,2]{1,2,0:T(2,128)} %copy.283), calls=%async_computation.8 | async-start | bytes 49152 | tf_op jit(solution)/shard_map/all_to_all | solution.py:87
  617.8 9.8 %all-to-all-start.9 = ((f32[4,24,2]{0,2,1:T(2,128)}), f32[4,24,2]{0,2,1:T(2,128)S(1)}, u32[]{:S(2)}, u32[]{:S(2)}) async-start(f32[4,24,2]{0,2,1:T(2,128)} %broadcast_select_fusion.2), calls=%async_computation.9 | async-start | bytes 49152 | tf_op jit(solution)/shard_map/all_to_all | solution.py:98
  627.7 9.7 %all-to-all-done.9 = f32[4,24,2]{0,2,1:T(2,128)S(1)} async-done(((f32[4,24,2]{0,2,1:T(2,128)}), f32[4,24,2]{0,2,1:T(2,128)S(1)}, u32[]{:S(2)}, u32[]{:S(2)}) %all-to-all-start.9) | async-done | bytes 800 | tf_op jit(solution)/shard_map/all_to_all | solution.py:98
  637.5 57.9 %all-reduce.4 = (f32[1,4,128]{2,1,0:T(4,128)S(1)}, f32[96,2]{0,1:T(2,128)S(1)}, f32[96,2]{0,1:T(2,128)S(1)}) all-reduce(f32[1,4,128]{2,1,0:T(4,128)S(1)} %select_bitcast_fusion.9, f32[96,2]{0,1:T(2,128)S(1)} %broadcast_multiply_fusion.2, f32[96,2]{0,1:T(2,128)S(1)} %all_to_all.230), channel_id=1, replica_groups=mesh['sub'=32,'col'=24] {'sub'}, use_global_device_ids=true, to_apply=%region_28.30 | all-reduce | flops 896 | bytes 7168 | tf_op jit(solution)/shard_map/psum | solution.py:100
  696.1 17.6 %all-to-all-start.10 = ((f32[24,4,2]{1,2,0:T(2,128)}), f32[24,4,2]{1,2,0:T(2,128)S(1)}, u32[]{:S(2)}, u32[]{:S(2)}) async-start(f32[24,4,2]{1,2,0:T(2,128)} %copy.295), calls=%async_computation.10 | async-start | bytes 49152 | tf_op jit(solution)/shard_map/all_to_all | solution.py:87
  730.5 9.8 %all-to-all-start.11 = ((f32[4,24,2]{0,2,1:T(2,128)}), f32[4,24,2]{0,2,1:T(2,128)S(1)}, u32[]{:S(2)}, u32[]{:S(2)}) async-start(f32[4,24,2]{0,2,1:T(2,128)} %broadcast_select_fusion.1), calls=%async_computation.11 | async-start | bytes 49152 | tf_op jit(solution)/shard_map/all_to_all | solution.py:98
  740.3 9.7 %all-to-all-done.11 = f32[4,24,2]{0,2,1:T(2,128)S(1)} async-done(((f32[4,24,2]{0,2,1:T(2,128)}), f32[4,24,2]{0,2,1:T(2,128)S(1)}, u32[]{:S(2)}, u32[]{:S(2)}) %all-to-all-start.11) | async-done | bytes 800 | tf_op jit(solution)/shard_map/all_to_all | solution.py:98
  750.1 56.1 %all-reduce.3 = (f32[1,4,128]{2,1,0:T(4,128)S(1)}, f32[96,2]{0,1:T(2,128)S(1)}, f32[96,2]{0,1:T(2,128)S(1)}) all-reduce(f32[1,4,128]{2,1,0:T(4,128)S(1)} %select_bitcast_fusion.8, f32[96,2]{0,1:T(2,128)S(1)} %broadcast_multiply_fusion.1, f32[96,2]{0,1:T(2,128)S(1)} %all_to_all.237), channel_id=1, replica_groups=mesh['sub'=32,'col'=24] {'sub'}, use_global_device_ids=true, to_apply=%region_34.36 | all-reduce | flops 896 | bytes 7168 | tf_op jit(solution)/shard_map/psum | solution.py:100
  806.9 17.5 %all-to-all-start.12 = ((f32[24,4,2]{1,2,0:T(2,128)}), f32[24,4,2]{1,2,0:T(2,128)S(1)}, u32[]{:S(2)}, u32[]{:S(2)}) async-start(f32[24,4,2]{1,2,0:T(2,128)} %copy.312), calls=%async_computation.12 | async-start | bytes 49152 | tf_op jit(solution)/shard_map/all_to_all | solution.py:87
  846.1 9.8 %all-to-all-start.13 = ((f32[4,24,2]{0,2,1:T(2,128)}), f32[4,24,2]{0,2,1:T(2,128)S(1)}, u32[]{:S(2)}, u32[]{:S(2)}) async-start(f32[4,24,2]{0,2,1:T(2,128)} %broadcast_select_fusion), calls=%async_computation.13 | async-start | bytes 49152 | tf_op jit(solution)/shard_map/all_to_all | solution.py:98
  857.5 8.1 all-to-all-done.13
  865.7 57.9 %all-reduce.2 = (f32[96,2]{0,1:T(2,128)S(1)}, f32[96,2]{0,1:T(2,128)S(1)}) all-reduce(f32[96,2]{0,1:T(2,128)S(1)} %broadcast_multiply_fusion, f32[96,2]{0,1:T(2,128)S(1)} %all_to_all.244), channel_id=1, replica_groups=mesh['sub'=32,'col'=24] {'sub'}, use_global_device_ids=true, to_apply=%region_40.42 | all-reduce | flops 384 | bytes 3072 | tf_op jit(solution)/shard_map/psum | solution.py:81
  924.4 17.6 %all-to-all-start.14 = ((f32[24,4,2]{1,2,0:T(2,128)}), f32[24,4,2]{1,2,0:T(2,128)S(1)}, u32[]{:S(2)}, u32[]{:S(2)}) async-start(f32[24,4,2]{1,2,0:T(2,128)} %copy.317), calls=%async_computation.14 | async-start | bytes 49152 | tf_op jit(solution)/shard_map/all_to_all | solution.py:87
  942.8 9.0 all-to-all-done.14
  (317 shorter events, 146.9 us)
Async XLA Ops:
  0.6 147.0 %copy-start = (bf16[2,64,2048]{2,1,0:T(8,128)(2,1)S(1)}, bf16[2,64,2048]{2,1,0:T(8,128)(2,1)}, u32[]{:S(2)}) copy-start(bf16[2,64,2048]{2,1,0:T(8,128)(2,1)} %param.44) | copy-start | bytes 1572868
  65.9 88.9 %all-to-all-start = ((f32[24,4,2]{1,2,0:T(2,128)}), f32[24,4,2]{1,2,0:T(2,128)S(1)}, u32[]{:S(2)}, u32[]{:S(2)}) async-start(f32[24,4,2]{1,2,0:T(2,128)} %copy.235), calls=%async_computation | async-start | bytes 49152 | tf_op jit(solution)/shard_map/all_to_all | solution.py:87
  101.1 10.6 %copy-start.4 = (s32[64,4]{0,1:T(4,128)S(1)}, s32[64,4]{0,1:T(4,128)}, u32[]{:S(2)}) copy-start(s32[64,4]{0,1:T(4,128)} %param.49) | copy-start | bytes 3076
  106.1 5.9 copy-start.7
  106.1 6.2 copy-start.5
  106.1 6.2 copy-start.3
  106.1 41.2 %copy-start.1 = (f32[96,2,75]{0,1,2:T(2,128)S(1)}, f32[96,2,75]{0,1,2:T(2,128)}, u32[]{:S(2)}) copy-start(f32[96,2,75]{0,1,2:T(2,128)} %param.54) | copy-start | bytes 172804
  156.4 91.8 %copy-start.2 = (s32[8,96,2]{1,2,0:T(2,128)S(1)}, s32[8,96,2]{1,2,0:T(2,128)}, u32[]{:S(2)}) copy-start(s32[8,96,2]{1,2,0:T(2,128)} %param.55) | copy-start | bytes 18436
  158.4 31.7 %all-to-all-start.1 = ((f32[4,24,2]{0,2,1:T(2,128)}), f32[4,24,2]{0,2,1:T(2,128)S(1)}, u32[]{:S(2)}, u32[]{:S(2)}) async-start(f32[4,24,2]{0,2,1:T(2,128)} %broadcast_select_fusion.6), calls=%async_computation.1 | async-start | bytes 49152 | tf_op jit(solution)/shard_map/all_to_all | solution.py:98
  249.0 30.6 %all-to-all-start.2 = ((f32[24,4,2]{1,2,0:T(2,128)}), f32[24,4,2]{1,2,0:T(2,128)S(1)}, u32[]{:S(2)}, u32[]{:S(2)}) async-start(f32[24,4,2]{1,2,0:T(2,128)} %copy.247), calls=%async_computation.2 | async-start | bytes 49152 | tf_op jit(solution)/shard_map/all_to_all | solution.py:87
  283.8 19.5 %all-to-all-start.3 = ((f32[4,24,2]{0,2,1:T(2,128)}), f32[4,24,2]{0,2,1:T(2,128)S(1)}, u32[]{:S(2)}, u32[]{:S(2)}) async-start(f32[4,24,2]{0,2,1:T(2,128)} %broadcast_select_fusion.5), calls=%async_computation.3 | async-start | bytes 49152 | tf_op jit(solution)/shard_map/all_to_all | solution.py:98
  360.2 30.0 %all-to-all-start.4 = ((f32[24,4,2]{1,2,0:T(2,128)}), f32[24,4,2]{1,2,0:T(2,128)S(1)}, u32[]{:S(2)}, u32[]{:S(2)}) async-start(f32[24,4,2]{1,2,0:T(2,128)} %copy.259), calls=%async_computation.4 | async-start | bytes 49152 | tf_op jit(solution)/shard_map/all_to_all | solution.py:87
  394.4 19.5 %all-to-all-start.5 = ((f32[4,24,2]{0,2,1:T(2,128)}), f32[4,24,2]{0,2,1:T(2,128)S(1)}, u32[]{:S(2)}, u32[]{:S(2)}) async-start(f32[4,24,2]{0,2,1:T(2,128)} %broadcast_select_fusion.4), calls=%async_computation.5 | async-start | bytes 49152 | tf_op jit(solution)/shard_map/all_to_all | solution.py:98
  472.7 30.1 %all-to-all-start.6 = ((f32[24,4,2]{1,2,0:T(2,128)}), f32[24,4,2]{1,2,0:T(2,128)S(1)}, u32[]{:S(2)}, u32[]{:S(2)}) async-start(f32[24,4,2]{1,2,0:T(2,128)} %copy.271), calls=%async_computation.6 | async-start | bytes 49152 | tf_op jit(solution)/shard_map/all_to_all | solution.py:87
  507.0 19.5 %all-to-all-start.7 = ((f32[4,24,2]{0,2,1:T(2,128)}), f32[4,24,2]{0,2,1:T(2,128)S(1)}, u32[]{:S(2)}, u32[]{:S(2)}) async-start(f32[4,24,2]{0,2,1:T(2,128)} %broadcast_select_fusion.3), calls=%async_computation.7 | async-start | bytes 49152 | tf_op jit(solution)/shard_map/all_to_all | solution.py:98
  583.4 30.2 %all-to-all-start.8 = ((f32[24,4,2]{1,2,0:T(2,128)}), f32[24,4,2]{1,2,0:T(2,128)S(1)}, u32[]{:S(2)}, u32[]{:S(2)}) async-start(f32[24,4,2]{1,2,0:T(2,128)} %copy.283), calls=%async_computation.8 | async-start | bytes 49152 | tf_op jit(solution)/shard_map/all_to_all | solution.py:87
  617.8 19.5 %all-to-all-start.9 = ((f32[4,24,2]{0,2,1:T(2,128)}), f32[4,24,2]{0,2,1:T(2,128)S(1)}, u32[]{:S(2)}, u32[]{:S(2)}) async-start(f32[4,24,2]{0,2,1:T(2,128)} %broadcast_select_fusion.2), calls=%async_computation.9 | async-start | bytes 49152 | tf_op jit(solution)/shard_map/all_to_all | solution.py:98
  696.1 30.1 %all-to-all-start.10 = ((f32[24,4,2]{1,2,0:T(2,128)}), f32[24,4,2]{1,2,0:T(2,128)S(1)}, u32[]{:S(2)}, u32[]{:S(2)}) async-start(f32[24,4,2]{1,2,0:T(2,128)} %copy.295), calls=%async_computation.10 | async-start | bytes 49152 | tf_op jit(solution)/shard_map/all_to_all | solution.py:87
  730.5 19.5 %all-to-all-start.11 = ((f32[4,24,2]{0,2,1:T(2,128)}), f32[4,24,2]{0,2,1:T(2,128)S(1)}, u32[]{:S(2)}, u32[]{:S(2)}) async-start(f32[4,24,2]{0,2,1:T(2,128)} %broadcast_select_fusion.1), calls=%async_computation.11 | async-start | bytes 49152 | tf_op jit(solution)/shard_map/all_to_all | solution.py:98
  806.9 35.6 %all-to-all-start.12 = ((f32[24,4,2]{1,2,0:T(2,128)}), f32[24,4,2]{1,2,0:T(2,128)S(1)}, u32[]{:S(2)}, u32[]{:S(2)}) async-start(f32[24,4,2]{1,2,0:T(2,128)} %copy.312), calls=%async_computation.12 | async-start | bytes 49152 | tf_op jit(solution)/shard_map/all_to_all | solution.py:87
  846.1 19.5 %all-to-all-start.13 = ((f32[4,24,2]{0,2,1:T(2,128)}), f32[4,24,2]{0,2,1:T(2,128)S(1)}, u32[]{:S(2)}, u32[]{:S(2)}) async-start(f32[4,24,2]{0,2,1:T(2,128)} %broadcast_select_fusion), calls=%async_computation.13 | async-start | bytes 49152 | tf_op jit(solution)/shard_map/all_to_all | solution.py:98
  923.7 30.3 %copy-start.6 = (f32[8,96,2]{1,2,0:T(2,128)}, f32[8,96,2]{1,2,0:T(2,128)S(1)}, u32[]{:S(2)}) copy-start(f32[8,96,2]{1,2,0:T(2,128)S(1)} %get-tuple-element.216) | copy-start | bytes 18436
  924.4 27.5 %all-to-all-start.14 = ((f32[24,4,2]{1,2,0:T(2,128)}), f32[24,4,2]{1,2,0:T(2,128)S(1)}, u32[]{:S(2)}, u32[]{:S(2)}) async-start(f32[24,4,2]{1,2,0:T(2,128)} %copy.317), calls=%async_computation.14 | async-start | bytes 49152 | tf_op jit(solution)/shard_map/all_to_all | solution.py:87
where the time goes:
time: 965 us; the launch traced here: 955 us
  blocking collectives  497 us (52%)
  starting transfers between devices  234 us (24%)
  local copies, waits for them, and re-layouts  107 us (11%)
  waiting for transfers between devices  74.7 us (8%)
  other arithmetic  35.9 us (4%)
    psum x6, blocking collectives, per_device(): lax.psum(end_part, 'sub')  342 us
    all_to_all x8, starting transfers between devices, per_device(): lax.all_to_all(current, 'col', split_axis=0, concat_axis=1, tiled=True)  154 us
    psum x2, blocking collectives, per_device(): thevenin, node_volt = lax.psum((thevenin_part, node_part), 'sub')  120 us
    all_to_all x7, starting transfers between devices, per_device(): lax.all_to_all(station_part, 'col', split_axis=1, concat_axis=0, tiled=True)  80.4 us
    all_to_all x7, waiting for transfers between devices, per_device(): lax.all_to_all(station_part, 'col', split_axis=1, concat_axis=0, tiled=True)  65.7 us
    gather x8, local copies, waits for them, and re-layouts, per_device(): volt_read = jnp.take_along_axis(volt_buffer, selector, axis=0)[0]  39.5 us
    gather x8, local copies, waits for them, and re-layouts, per_device(): inj_read = jnp.take_along_axis(inj_buffer, selector, axis=0)[0]  39.5 us
    all_gather x1, blocking collectives, per_device(): lax.all_gather(source, 'sub', axis=2, tiled=True)  34.8 us
  transfers between devices with their start and end apart: 15, of which 8 were waited for; matrix products, arithmetic and copies ran while one was open for 11% of the time, Pallas kernels for 0%

commit v1 on v0

v1 whole, which is shorter than its diff:
```python
import jax
import jax.numpy as jnp
from jax import lax
from jax.experimental import pallas as pl
from jax.experimental.pallas import tpu as pltpu
from jax.sharding import PartitionSpec as P

SM = 2400
STEPS = 8
DMIN = 2
DMAX = 6
NS = 2048
NX, NY, NC = 4, 8, 24
F32, BF16 = jnp.float32, jnp.bfloat16
MESH = pl.DeviceIdType.MESH
NT = (((1,), (1,)), ((), ()))


def split3(x):
    hi = x.astype(BF16).astype(F32)
    rest = x - hi
    mid = rest.astype(BF16).astype(F32)
    return hi, mid, rest - mid


def dot(a, b):
    return jnp.dot(a, b, preferred_element_type=F32)


def exact_dot(x, onehot):
    parts = jnp.concatenate([*split3(x), jnp.zeros_like(x)], axis=0)
    r = dot(parts.astype(BF16), onehot)
    return r[0:4] + r[4:8] + r[8:12]


def kernel(
    inv_ref, src_ref, ncol_ref, nrow_ref, msg0_ref, hv_ref, hj_ref, mask_ref, line_ref,
    volt_ref, cur_ref,
    gt_ref, s_ref, t_ref, send1y, buf1y, send1x, buf1x, wsend, wbuf, buf0, send2y, buf2y, send2x, buf2x, send3,
    s0, r0, s1y, r1y, s1x, r1x, sw, rw, s2y, r2y, s2x, r2x, s3, r3,
):
    sub, col = lax.axis_index("sub"), lax.axis_index("col")
    y, x = sub // NX, lax.rem(sub, NX)
    to_y = lambda p: {"sub": p * NX + x}
    to_x = lambda p: {"sub": y * NX + p}
    to_c = lambda p: {"col": p}

    def push(n, me, to, src, dst, send, recv):
        def body(d, carry):
            p = lax.rem(me + d, n)
            pltpu.make_async_remote_copy(
                src_ref=src(p), dst_ref=dst.at[me], send_sem=send.at[p], recv_sem=recv.at[me],
                device_id=to(p), device_id_type=MESH,
            ).start()
            return carry

        lax.fori_loop(1, n, body, 0)

    def copy_of(to, src, dst, send, recv, p):
        return pltpu.make_async_remote_copy(
            src_ref=src(p), dst_ref=dst.at[p], send_sem=send.at[p], recv_sem=recv.at[p],
            device_id=to(p), device_id_type=MESH,
        )

    def await_recv(n, me, to, src, dst, send, recv):
        def body(d, carry):
            copy_of(to, src, dst, send, recv, lax.rem(me + d, n)).wait_recv()
            return carry

        lax.fori_loop(1, n, body, 0)

    def await_send(n, me, to, src, dst, send, recv):
        def body(d, carry):
            copy_of(to, src, dst, send, recv, lax.rem(me + d, n)).wait_send()
            return carry

        lax.fori_loop(1, n, body, 0)

    barrier = pltpu.get_barrier_semaphore()
    for n, me, to in ((NC, col, to_c), (NY, y, to_y), (NX, x, to_x)):

        def greet(d, carry, n=n, me=me, to=to):
            pl.semaphore_signal(
                barrier, inc=1, device_id=to(lax.rem(me + d, n)), device_id_type=MESH
            )
            return carry

        lax.fori_loop(1, n, greet, 0)

    lane = lax.broadcasted_iota(jnp.int32, (1, 128), 1)
    low = lane < 64
    ncol = ncol_ref[...]
    ends_row, st_row = nrow_ref[:, 0:128], nrow_ref[:, 128:256]

    place = lax.rem(ncol[0:192], NS)
    acc = jnp.zeros((192, 128), F32)
    for k in range(0, NS, 512):
        spot = lax.broadcasted_iota(jnp.int32, (192, 512), 1) + k
        onehot = jnp.where(place == spot, 1.0, 0.0).astype(BF16)
        acc += lax.dot_general(onehot, inv_ref[:, k : k + 512], NT, preferred_element_type=F32)
    same_sub = jnp.where(ncol[0:192] >= NS, 1, 0) == jnp.where(low, 0, 1)
    gt = jnp.where(same_sub, acc, 0.0)
    gt_ref[...] = gt

    r = lax.broadcasted_iota(jnp.int32, (128, 1), 0)
    gid = jnp.where(r >= 64, NS - 64, 0) + r + sub * 64
    st_high = pltpu.roll(st_row, 64, 1)
    row0 = jnp.where(low, ends_row, st_high)
    row1 = jnp.where(low, pltpu.roll(ends_row, 64, 1), st_high)
    pick = jnp.where(gid == jnp.where(r >= 64, row1, row0), 1.0, 0.0).astype(BF16)
    mine = gt_ref[pl.ds(pl.multiple_of(col * 8, 8), 8), :]
    send1y[0:8, :] = dot(mine.astype(BF16), pick)
    send1y[8:12, :] = src_ref[...]
    send1y[12:16, :] = jnp.zeros((4, 128), F32)
    pl.semaphore_wait(barrier, NC + NY + NX - 3)

    ex1y = (NY, y, to_y, lambda p: send1y, buf1y, s1y, r1y)
    ex0 = (NC, col, to_c, lambda p: msg0_ref.at[p], buf0, s0, r0)
    push(*ex1y)
    push(*ex0)
    buf1y[y] = send1y[...]
    buf0[col] = msg0_ref[col]

    b_row = lax.broadcasted_iota(jnp.int32, (256, 256), 0)
    b_col = lax.broadcasted_iota(jnp.int32, (256, 256), 1)
    equal = ncol == nrow_ref[...]
    earlier = jnp.where(equal & (b_row < b_col), 1.0, 0.0)
    first = jnp.sum(earlier, axis=0, keepdims=True) == 0.0
    merge = jnp.where(equal & first, 1.0, 0.0).astype(BF16)
    at_ends = jnp.where(gid == ends_row, 1.0, 0.0).astype(BF16)
    at_st = jnp.where(gid == st_row, 1.0, 0.0).astype(BF16)

    await_recv(*ex1y)
    total = buf1y[0, 0:8]
    for p in range(1, NY):
        total += buf1y[p, 0:8]
    send1x[0:8, :] = total
    for p in range(NY):
        send1x[8 + 4 * p : 12 + 4 * p, :] = buf1y[p, 8:12]
    ex1x = (NX, x, to_x, lambda p: send1x, buf1x, s1x, r1x)
    push(*ex1x)
    buf1x[x] = send1x[...]

    await_recv(*ex0)
    t_ref[...] = jnp.zeros((128, 128), F32)
    for p in range(NC):
        t_ref[2 * p : 2 * p + 2, :] = buf0[p]
    stations = t_ref[...].T
    packed = jnp.where(low, stations[0:16], pltpu.roll(stations[16:32], 64, 1))

    await_recv(*ex1x)
    block = buf1x[0, 0:8]
    for p in range(1, NX):
        block += buf1x[p, 0:8]
    wsend[...] = block
    exw = (NC, col, to_c, lambda p: wsend, wbuf, sw, rw)
    push(*exw)
    wbuf[col] = block
    for p in range(NY):
        for q in range(NX // 2):
            a = buf1x[2 * q, 8 + 4 * p : 12 + 4 * p]
            b = buf1x[2 * q + 1, 8 + 4 * p : 12 + 4 * p]
            m = (2 * p + q) * 128
            s_ref[0:4, m : m + 128] = jnp.where(low, a, pltpu.roll(b, 64, 1))
            s_ref[4:8, m : m + 128] = jnp.where(low, pltpu.roll(a, 64, 1), b)
    both = lax.dot_general(s_ref[...].astype(BF16), inv_ref[...], NT, preferred_element_type=F32)
    source_part = jnp.where(low, both[0:4], both[4:8])
    send2y[0:16, :] = packed
    send2y[16:20, :] = exact_dot(source_part, at_ends)
    send2y[20:24, :] = exact_dot(source_part, at_st)
    ex2y = (NY, y, to_y, lambda p: send2y, buf2y, s2y, r2y)
    push(*ex2y)
    buf2y[y] = send2y[...]

    await_recv(*ex2y)
    total = buf2y[0]
    for p in range(1, NY):
        total += buf2y[p]
    send2x[...] = total
    ex2x = (NX, x, to_x, lambda p: send2x, buf2x, s2x, r2x)
    push(*ex2x)
    buf2x[x] = total

    await_recv(*exw)
    w = jnp.concatenate([wbuf[p] for p in range(NC)], axis=0)
    high_w = pltpu.roll(w, 64, 1)
    is_high = ncol[0:192] >= NS
    w_ends = jnp.where(low, jnp.where(is_high, 0.0, w), jnp.where(is_high, high_w, 0.0))
    w_st = jnp.where(low, high_w, 0.0)
    w_full = jnp.concatenate(
        [jnp.concatenate([w_ends, w_st], axis=1), jnp.zeros((64, 256), F32)], axis=0
    ).astype(BF16)

    await_recv(*ex2x)
    total = buf2x[0]
    for p in range(1, NX):
        total += buf2x[p]
    station_lane = lane < 48
    sums = jnp.where(
        station_lane,
        jnp.concatenate([total[0:16], pltpu.roll(total[0:16], 64, 1)], axis=0),
        0.0,
    )
    src_nodes = jnp.concatenate([total[16:20], total[20:24]], axis=1)

    volts = [hv_ref[t] for t in range(DMAX)]
    injs = [hj_ref[t] for t in range(DMAX)]
    counts = [jnp.where(station_lane, stations[32 + 4 * n : 36 + 4 * n], 0.0) for n in range(STEPS)]
    node_volt = jnp.where(station_lane, stations[64:68], 0.0)
    delay = line_ref[0:1, :]
    twice = 2.0 * line_ref[1:2, :]
    in_service = mask_ref[...]
    currents = []
    for n in range(STEPS):
        u, j = volts[n + DMAX - DMIN], injs[n + DMAX - DMIN]
        for d in range(DMIN + 1, DMAX + 1):
            at = delay == float(d)
            u = jnp.where(at, volts[n + DMAX - d], u)
            j = jnp.where(at, injs[n + DMAX - d], j)
        injection = in_service * (twice * pltpu.roll(u, 64, 1) - pltpu.roll(j, 64, 1))
        injs.append(injection)
        charge = sums[4 * n : 4 * n + 4]
        for q in range(n):
            charge -= 0.5 * jnp.minimum(counts[n], counts[q]) * currents[q]
        current = (2.0 / SM * charge - node_volt) / (1.0 + counts[n] / SM)
        current = jnp.where(station_lane, current, 0.0)
        currents.append(current)
        term = exact_dot(jnp.concatenate([injection, current], axis=1), merge)
        term = jnp.concatenate([term, jnp.zeros_like(term)], axis=0).astype(BF16)
        if n + 1 < STEPS:
            nodes = dot(term, w_full)[0:4] + src_nodes
            volts.append(nodes[:, 0:128])
            node_volt = nodes[:, 128:256]

    t_ref[0:32, :] = jnp.concatenate(currents, axis=0)
    t_ref[32:128, :] = jnp.zeros((96, 128), F32)
    out = t_ref[...].T
    for p in range(NC):
        send3[p] = out[2 * p : 2 * p + 2, :]
    ex3 = (NC, col, to_c, lambda p: send3.at[p], cur_ref, s3, r3)
    push(*ex3)
    cur_ref[col] = send3[col]
    last = dot(term, jnp.concatenate([gt, jnp.zeros((64, 128), F32)], axis=0).astype(BF16))
    volt_ref[...] = source_part + last[0:4]
    for ex in (ex0, ex1y, ex1x, exw, ex2y, ex2x):
        await_send(*ex)
    await_recv(*ex3)
    await_send(*ex3)


def exchange(inv, src, ncol, nrow, msg0, hv, hj, mask, line):
    vmem = pl.BlockSpec(memory_space=pltpu.VMEM)
    pairs = lambda n: [pltpu.SemaphoreType.DMA((n,)), pltpu.SemaphoreType.DMA((n,))]
    return pl.pallas_call(
        kernel,
        out_shape=(jax.ShapeDtypeStruct((4, 128), F32), jax.ShapeDtypeStruct((NC, 2, 128), F32)),
        in_specs=[vmem] * 9,
        out_specs=(vmem, vmem),
        scratch_shapes=[
            pltpu.VMEM((192, 128), F32),
            pltpu.VMEM((8, NS), F32),
            pltpu.VMEM((128, 128), F32),
            pltpu.VMEM((16, 128), F32),
            pltpu.VMEM((NY, 16, 128), F32),
            pltpu.VMEM((40, 128), F32),
            pltpu.VMEM((NX, 40, 128), F32),
            pltpu.VMEM((8, 128), F32),
            pltpu.VMEM((NC, 8, 128), F32),
            pltpu.VMEM((NC, 2, 128), F32),
            pltpu.VMEM((24, 128), F32),
            pltpu.VMEM((NY, 24, 128), F32),
            pltpu.VMEM((24, 128), F32),
            pltpu.VMEM((NX, 24, 128), F32),
            pltpu.VMEM((NC, 2, 128), F32),
            *pairs(NC), *pairs(NY), *pairs(NX), *pairs(NC), *pairs(NY), *pairs(NX), *pairs(NC),
        ],
        compiler_params=pltpu.CompilerParams(
            collective_id=0, has_side_effects=True, vmem_limit_bytes=24 * 1024 * 1024
        ),
    )(inv, src, ncol, nrow, msg0, hv, hj, mask, line)


def per_device(
    inv_conductance, source, line_ends, delays, admittance, breaker, hist_volt, hist_inj,
    station_node, station_initial, capacitor_initial, insert_count,
):
    sub_index = lax.axis_index("sub")
    flip = line_ends[:, 0] >= NS
    low_end = jnp.where(flip, line_ends[:, 1], line_ends[:, 0])
    high_end = jnp.where(flip, line_ends[:, 0], line_ends[:, 1])
    node = jnp.concatenate([low_end, high_end, station_node, -1 - jnp.arange(80, dtype=jnp.int32)])

    def by_sub(hist):
        paired = hist.reshape(DMAX, 4, 64, 2)
        even, odd = paired[..., 0], paired[..., 1]
        return jnp.concatenate([jnp.where(flip, odd, even), jnp.where(flip, even, odd)], axis=-1)

    mask = breaker.T.astype(F32)
    mask = jnp.concatenate([mask, mask], axis=1)
    line = jnp.stack([delays.astype(F32), admittance])
    line = jnp.concatenate([line, line], axis=1)

    position = sub_index * 75 + jnp.arange(75, dtype=jnp.int32)
    inserted = position < insert_count[..., None]
    part = jnp.sum(jnp.where(inserted, capacitor_initial, 0.0), axis=-1)
    to_owner = lambda v: v.reshape(STEPS, NC, 4, 2).transpose(1, 3, 0, 2).reshape(NC, 2, 32)
    first = station_initial.reshape(NC, 4, 2).transpose(0, 2, 1)
    msg0 = jnp.concatenate(
        [to_owner(part), to_owner(insert_count.astype(F32)), first, jnp.zeros((NC, 2, 60), F32)], axis=-1
    )
    volts, currents = exchange(
        inv_conductance.reshape(128, NS), source.astype(F32).reshape(4, 128), node[:, None], node[None, :],
        msg0, by_sub(hist_volt), by_sub(hist_inj), mask, line,
    )
    current = currents[:, :, :32].reshape(NC, 2, STEPS, 4).transpose(2, 0, 3, 1).reshape(STEPS, 96, 2)
    capacitor = capacitor_initial - 0.5 * jnp.sum(jnp.where(inserted, current[..., None], 0.0), axis=0)
    return volts.reshape(4, 2, 64), capacitor, current


def solution(mesh):
    in_specs = (
        P(None, "sub", None),
        P("col", None, "sub"),
        P(),
        P(),
        P(),
        P(None, "col"),
        P(None, "col", None),
        P(None, "col", None),
        P(),
        P(None, "col"),
        P(None, "col", "sub"),
        P(None, None, "col"),
    )
    out_specs = (P("col", None, "sub"), P(None, "col", "sub"), P(None, None, "col"))
    return jax.shard_map(
        per_device, mesh=mesh, in_specs=in_specs, out_specs=out_specs, check_vma=False
    )
```

time: 965 us -> 59.9 us (0.06)
  blocking collectives: 497 us -> 0 us
  starting transfers between devices: 234 us -> 0 us
  local copies, waits for them, and re-layouts: 107 us -> 10.6 us
  waiting for transfers between devices: 74.7 us -> 0 us
  Pallas kernels: 0 us -> 47.1 us
  other arithmetic: 35.9 us -> 0.92 us
    psum x8 -> x0, blocking collectives: 462 us -> none  [the longest x6 342 us: per_device(): lax.psum(end_part, 'sub')]
    all_to_all x15 -> x0, starting transfers between devices: 234 us -> none  [the longest x8 154 us: per_device(): lax.all_to_all(current, 'col', split_axis=0, concat_axis=1, tiled=True)]
    gather x35 -> x0, local copies, waits for them, and re-layouts: 87.4 us -> none  [the longest x8 39.5 us: per_device(): volt_read = jnp.take_along_axis(volt_buffer, selector, axis=0)[0]]
    all_to_all x15 -> x0, waiting for transfers between devices: 74.7 us -> none  [the longest x7 65.7 us: per_device(): lax.all_to_all(station_part, 'col', split_axis=1, concat_axis=0, tiled=True)]
    pallas_call x0 -> x1, Pallas kernels: none -> 47.1 us  [exchange(): pl.pallas_call(kernel, out_shape=(jax.ShapeDtypeStruct((4, 128), F32), ja...]
    all_gather x1 -> x0, blocking collectives: 34.8 us -> none  [per_device(): lax.all_gather(source, 'sub', axis=2, tiled=True)]
    scatter-add x16 -> x0, other arithmetic: 25.1 us -> none  [per_device(): term_full.at[:, end_nodes].add(injection).at[:, station_node]]
  transfers between devices with their start and end apart: 15 -> 0, of which waited for: 8 -> 0; matrix products, arithmetic and copies ran while one was open for 11% -> 0% of each run, Pallas kernels for 0% -> 0%
where the time goes in v1:
time: 59.9 us; the launch traced here: 59.5 us
  Pallas kernels  47.1 us (79%)
  local copies, waits for them, and re-layouts  10.6 us (18%)
  other arithmetic  0.92 us (2%)
  between operations  0.8 us (1%)
    pallas_call x1, Pallas kernels, exchange(): pl.pallas_call(kernel, out_shape=(jax.ShapeDtypeStruct((4, 128), F32), ja...  47.1 us
    unnamed x32, local copies, waits for them, and re-layouts  8.32 us

profile of v1, /device:TPU:1, one launch (start us, length us, event | category | flops | bytes accessed | tf_op | source)
XLA Modules:
  0.0 59.5 jit_solution(1988913934695710708)
XLA Ops:
  0.6 0.8 %copy.48 = f32[6,4,128]{0,2,1:T(8,128)S(1)} copy(f32[6,4,128]{2,1,0:T(4,128)} %param.18) | data formatting | bytes 24576 | tf_op args[6]
  1.5 0.2 fusion.3
  1.7 0.1 copy.61
  1.8 0.1 copy.62
  1.9 0.6 %copy-done.3 = f32[6,4,128]{2,1,0:T(4,128)S(1)} copy-done((f32[6,4,128]{2,1,0:T(4,128)S(1)}, f32[6,4,128]{2,1,0:T(4,128)}, u32[]{:S(2)}) %copy-start.3) | copy-done | bytes 12312
  2.5 0.1 copy.51
  2.7 0.2 fusion.2
  2.9 0.1 copy.63
  3.0 0.1 copy.64
  3.1 0.6 copy-done.7
  3.8 0.6 %copy-done.8 = s32[48]{0:T(128)S(1)} copy-done((s32[48]{0:T(128)S(1)}, s32[48]{0:T(128)}, u32[]{:S(2)}) %copy-start.8) | copy-done | bytes 216
  4.5 0.1 copy.54.ncol_ref
  4.6 0.6 copy-done.2
  5.2 0.2 copy-done.1
  5.4 0.1 fusion
  5.6 0.1 copy.41
  5.7 0.1 copy.42
  5.9 0.1 copy.43
  6.0 0.1 copy.44
  6.1 0.1 copy.47
  6.2 0.6 %copy-done.6 = f32[96,2]{0,1:T(2,128)S(1)} copy-done((f32[96,2]{0,1:T(2,128)S(1)}, f32[96,2]{0,1:T(2,128)}, u32[]{:S(2)}) %copy-start.6) | copy-done | bytes 792
  7.0 0.1 maximum_maximum_fusion.msg0_ref
  7.1 0.6 copy-done.4
  7.8 0.6 %copy-done.5 = bf16[4,2,64]{2,1,0:T(2,128)(2,1)S(1)} copy-done((bf16[4,2,64]{2,1,0:T(2,128)(2,1)S(1)}, bf16[4,2,64]{2,1,0:T(2,128)(2,1)}, u32[]{:S(2)}) %copy-start.5) | copy-done | bytes 1048
  8.5 0.6 copy-done.10
  9.0 0.7 %copy-done.9 = f32[64]{0:T(128)S(1)} copy-done((f32[64]{0:T(128)S(1)}, f32[64]{0:T(128)}, u32[]{:S(2)}) %copy-start.9) | copy-done | bytes 280
  9.8 47.1 %shard_map.139 = (f32[4,128]{1,0:T(4,128)S(1)}, f32[24,2,128]{2,1,0:T(2,128)S(1)}) custom-call(bf16[128,2048]{1,0:T(8,128)(2,1)S(1)} %bitcast.51, f32[4,128]{1,0:T(4,128)S(1)} %reshape.61.src_ref, s32[256,1]{1,0:T(8,128)S(1)} %copy.54.ncol_ref, s32[1,256]{1,0:T(1,128)S(1)} %bitcast.54, f32[24,2,128]{2,1,0:T(2,128)S(1)} %maximum_maximum_fusion.msg0_ref, ...), custom_call_target="tpu_custom_call" | custom-call | tf_op jit(solution)/shard_map/pallas_call | solution.py:254
  57.0 0.1 copy.56
  57.2 0.3 fusion.1
  57.5 0.7 %copy.59 = f32[96,2,75]{0,1,2:T(2,128)} copy(f32[96,2,75]{0,2,1:T(8,128)S(1)} %multiply_subtract_fusion) | data formatting | bytes 115200
  58.2 0.7 %copy.60 = f32[8,96,2]{1,2,0:T(2,128)} copy(f32[8,96,2]{0,1,2:T(8,128)S(1)} %bitcast.58) | data formatting | bytes 12288
  58.8 0.7 %reshape.58 = f32[4,2,64]{2,1,0:T(2,128)} reshape(f32[4,128]{1,0:T(4,128)S(1)} %get-tuple-element.5) | data formatting | bytes 4096 | tf_op jit(solution)/shard_map/reshape | solution.py:317
  (35 shorter events, 0.9 us)
Async XLA Ops:
  1.8 0.7 %copy-start.3 = (f32[6,4,128]{2,1,0:T(4,128)S(1)}, f32[6,4,128]{2,1,0:T(4,128)}, u32[]{:S(2)}) copy-start(f32[6,4,128]{2,1,0:T(4,128)} %param.19) | copy-start | bytes 36868
  3.0 0.7 %copy-start.7 = (s32[64,2]{0,1:T(2,128)S(1)}, s32[64,2]{0,1:T(2,128)}, u32[]{:S(2)}) copy-start(s32[64,2]{0,1:T(2,128)} %param.14) | copy-start | bytes 1540
  3.8 0.7 %copy-start.8 = (s32[48]{0:T(128)S(1)}, s32[48]{0:T(128)}, u32[]{:S(2)}) copy-start(s32[48]{0:T(128)} %param.20) | copy-start | bytes 580
  4.5 0.7 %copy-start.2 = (s32[8,96,2]{1,2,0:T(2,128)S(1)}, s32[8,96,2]{1,2,0:T(2,128)}, u32[]{:S(2)}) copy-start(s32[8,96,2]{1,2,0:T(2,128)} %param.23) | copy-start | bytes 18436
  4.5 0.9 %copy-start.1 = (f32[96,2,75]{0,1,2:T(2,128)S(1)}, f32[96,2,75]{0,1,2:T(2,128)}, u32[]{:S(2)}) copy-start(f32[96,2,75]{0,1,2:T(2,128)} %param.22) | copy-start | bytes 172804
  5.4 4.4 %copy-start = (bf16[2,64,2048]{2,1,0:T(8,128)(2,1)S(1)}, bf16[2,64,2048]{2,1,0:T(8,128)(2,1)}, u32[]{:S(2)}) copy-start(bf16[2,64,2048]{2,1,0:T(8,128)(2,1)} %param.12) | copy-start | bytes 1572868
  6.1 0.7 %copy-start.6 = (f32[96,2]{0,1:T(2,128)S(1)}, f32[96,2]{0,1:T(2,128)}, u32[]{:S(2)}) copy-start(f32[96,2]{0,1:T(2,128)} %param.21) | copy-start | bytes 2308
  7.0 0.7 %copy-start.4 = (s32[64,4]{0,1:T(4,128)S(1)}, s32[64,4]{0,1:T(4,128)}, u32[]{:S(2)}) copy-start(s32[64,4]{0,1:T(4,128)} %param.17) | copy-start | bytes 3076
  7.7 0.7 %copy-start.5 = (bf16[4,2,64]{2,1,0:T(2,128)(2,1)S(1)}, bf16[4,2,64]{2,1,0:T(2,128)(2,1)}, u32[]{:S(2)}) copy-start(bf16[4,2,64]{2,1,0:T(2,128)(2,1)} %param.13) | copy-start | bytes 3076
  8.4 0.7 %copy-start.10 = (s32[64]{0:T(128)S(1)}, s32[64]{0:T(128)}, u32[]{:S(2)}) copy-start(s32[64]{0:T(128)} %param.15) | copy-start | bytes 772
  9.0 0.7 %copy-start.9 = (f32[64]{0:T(128)S(1)}, f32[64]{0:T(128)}, u32[]{:S(2)}) copy-start(f32[64]{0:T(128)} %param.16) | copy-start | bytes 772

commit v2 on v1

v2 whole, which is shorter than its diff:
```python
import jax
import jax.numpy as jnp
from jax import lax
from jax.experimental import pallas as pl
from jax.experimental.pallas import tpu as pltpu
from jax.sharding import PartitionSpec as P

SM = 2400
STEPS = 8
DMIN = 2
DMAX = 6
NS = 2048
NX, NY, NC = 4, 8, 24
F32, BF16 = jnp.float32, jnp.bfloat16
MESH = pl.DeviceIdType.MESH
HBM = pltpu.MemorySpace.HBM
NT = (((1,), (1,)), ((), ()))


def split3(x):
    hi = x.astype(BF16).astype(F32)
    rest = x - hi
    mid = rest.astype(BF16).astype(F32)
    return hi, mid, rest - mid


def dot(a, b):
    return jnp.dot(a, b, preferred_element_type=F32)


def exact_dot(x, onehot):
    parts = jnp.concatenate([*split3(x), jnp.zeros_like(x)], axis=0)
    r = dot(parts.astype(BF16), onehot)
    return r[0:4] + r[4:8] + r[8:12]


def kernel(
    inv_hbm, src_in, ends_hbm, delay_hbm, admit_hbm, breaker_hbm, hv_hbm, hj_hbm, node_hbm, init_hbm, cap_hbm, count_hbm,
    volt_ref, cap_out, cur_out,
    inv_ref, ends_ref, delay_ref, admit_ref, breaker_ref, hv_ref, hj_ref, node_ref, init_ref, cap_ref, count_ref,
    gt_ref, s_ref, t_ref, q_ref, send1y, buf1y, send1x, buf1x, wsend, wbuf, msg0, buf0, send2y, buf2y, send2x, buf2x, send3, buf3,
    loads, s0, r0, s1y, r1y, s1x, r1x, sw, rw, s2y, r2y, s2x, r2x, s3, r3,
):
    sub, col = lax.axis_index("sub"), lax.axis_index("col")
    y, x = sub // NX, lax.rem(sub, NX)
    z, core = col // 2, lax.rem(col, 2)
    to_y = lambda p: {"sub": p * NX + x}
    to_x = lambda p: {"sub": y * NX + p}
    to_c = lambda p: {"col": p}

    def ring(n, me, to, src, dst, send, recv):
        return [
            (to(p), p, me, src(p), dst, send, recv) for p in [lax.rem(me + d, n) for d in range(1, n)]
        ]

    def copies(exchange):
        return [
            pltpu.make_async_remote_copy(
                src_ref=src, dst_ref=dst.at[there], send_sem=send.at[here], recv_sem=recv.at[there],
                device_id=device, device_id_type=MESH,
            )
            for device, here, there, src, dst, send, recv in exchange
        ]

    def push(exchange):
        for copy in copies(exchange):
            copy.start()

    def await_send(exchange):
        for copy in copies(exchange):
            copy.wait_send()

    def await_recv(exchange):
        for device, here, there, src, dst, send, recv in exchange:
            pltpu.make_async_remote_copy(
                src_ref=src, dst_ref=dst.at[here], send_sem=send.at[here], recv_sem=recv.at[here],
                device_id=device, device_id_type=MESH,
            ).wait_recv()

    fetches = [
        pltpu.make_async_copy(a, b, loads.at[i])
        for i, (a, b) in enumerate(
            [
                (ends_hbm, ends_ref), (node_hbm, node_ref), (inv_hbm, inv_ref), (cap_hbm, cap_ref),
                (count_hbm, count_ref), (init_hbm, init_ref), (delay_hbm, delay_ref), (admit_hbm, admit_ref),
                (breaker_hbm, breaker_ref), (hv_hbm, hv_ref), (hj_hbm, hj_ref),
            ]
        )
    ]
    for fetch in fetches:
        fetch.start()
    barrier = pltpu.get_barrier_semaphore()
    for n, me, to in ((NY, y, to_y), (NX, x, to_x), (NC, col, to_c)):
        for d in range(1, n):
            pl.semaphore_signal(
                barrier, inc=1, device_id=to(lax.rem(me + d, n)), device_id_type=MESH
            )

    lane = lax.broadcasted_iota(jnp.int32, (1, 128), 1)
    row = lax.broadcasted_iota(jnp.int32, (128, 1), 0)
    low = lane < 64
    station_lane = lane < 48
    twice_over = lambda v: jnp.concatenate([v, v], axis=1)

    fetches[0].wait()
    fetches[1].wait()
    e0, e1 = ends_ref[0:1, :], ends_ref[1:2, :]
    flip = e0 >= NS
    ends_row = jnp.concatenate([jnp.where(flip, e1, e0), jnp.where(flip, e0, e1)], axis=1)
    st_row = jnp.concatenate([node_ref[...], jnp.zeros((1, 80), jnp.int32)], axis=1)
    st_row = jnp.where(station_lane, st_row, -1 - lane)
    ends_col = jnp.broadcast_to(ends_row, (128, 128)).T
    st_col = jnp.broadcast_to(st_row, (128, 128)).T
    col192 = jnp.concatenate([ends_col, st_col[0:64]], axis=0)

    place = lax.rem(col192, NS)
    fetches[2].wait()
    acc = jnp.zeros((192, 128), F32)
    for k in range(0, NS, 256):
        halves = [jnp.where(place == lane + (k + h), 1.0, 0.0).astype(BF16) for h in (0, 128)]
        acc += lax.dot_general(
            jnp.concatenate(halves, axis=1), inv_ref[:, k : k + 256], NT, preferred_element_type=F32
        )
    gt = jnp.where((col192 >= NS) == jnp.broadcast_to(lane >= 64, (192, 128)), acc, 0.0)
    gt_ref[...] = gt

    gid = jnp.where(row >= 64, NS - 64, 0) + row + sub * 64
    st_high = pltpu.roll(st_row, 64, 1)
    row0 = jnp.where(low, ends_row, st_high)
    row1 = jnp.where(low, pltpu.roll(ends_row, 64, 1), st_high)
    pick = jnp.where(gid == jnp.where(row >= 64, row1, row0), 1.0, 0.0).astype(BF16)
    piece = lax.rem(z, 6) * 2 + core
    mine = gt_ref[pl.ds(pl.multiple_of(piece * 16, 16), 16), :]
    for c in range(4):
        pair = src_in[c].astype(F32)
        s_ref[c : c + 1, 0:128] = jnp.concatenate([pair[0:1], pair[1:2]], axis=1)
    first_part = [dot(mine.astype(BF16), pick), s_ref[0:4, 0:128], jnp.zeros((12, 128), F32)]
    send1y[...] = jnp.concatenate(first_part, axis=0).astype(BF16)
    pl.semaphore_wait(barrier, NC + NY + NX - 3)

    ex1y = ring(NY, y, to_y, lambda p: send1y, buf1y, s1y, r1y)
    push(ex1y)
    buf1y[y] = send1y[...]

    for i in (3, 4, 5):
        fetches[i].wait()
    position = lax.broadcasted_iota(jnp.int32, (75, 1, 1), 0) + sub * 75
    q_ref[...] = jnp.zeros((40, 128), F32)
    for n in range(STEPS):
        count = count_ref[n]
        part = jnp.sum(jnp.where(position < count[None], cap_ref[...], 0.0), axis=0)
        q_ref[2 * n : 2 * n + 2, 0:96] = part
        q_ref[16 + 2 * n : 18 + 2 * n, 0:96] = count.astype(F32)
    q_ref[32:34, 0:96] = init_ref[...]
    row48 = lax.broadcasted_iota(jnp.int32, (48, 1), 0)
    owner = lane // 4 == row48 // 2
    second = lax.rem(row48, 2) == 1
    moved = jnp.zeros((144, 128), F32)
    for q in range(0, 18, 2):
        wide, fold = [], []
        for h in (q, q + 1):
            v = jnp.where(second, q_ref[2 * h + 1 : 2 * h + 2, :], q_ref[2 * h : 2 * h + 1, :])
            wide.append(jnp.concatenate(split3(jnp.where(owner, v, 0.0)), axis=0).astype(BF16))
            fold.append(jnp.where(lane == 4 * h + lax.rem(row, 4), 1.0, 0.0).astype(BF16))
        moved += dot(jnp.concatenate(wide, axis=1), jnp.concatenate(fold, axis=0))
    moved = moved[0:48] + moved[48:96] + moved[96:144]
    for p in range(NC):
        msg0[p] = moved[2 * p : 2 * p + 2]
    ex0 = ring(NC, col, to_c, lambda p: msg0.at[p], buf0, s0, r0)
    push(ex0)
    buf0[col] = msg0[col]

    await_recv(ex1y)
    parts = [buf1y[p].astype(F32) for p in range(NY)]
    total = parts[0][0:16]
    for part in parts[1:]:
        total += part[0:16]
    send1x[...] = jnp.concatenate([total] + [part[16:20] for part in parts], axis=0).astype(BF16)
    ex1x = ring(NX, x, to_x, lambda p: send1x, buf1x, s1x, r1x)
    push(ex1x)
    buf1x[x] = send1x[...]

    nrow = jnp.concatenate([ends_row, st_row], axis=1)
    ncol = jnp.concatenate([twice_over(ends_col), twice_over(st_col)], axis=0)
    b_row = lax.broadcasted_iota(jnp.int32, (256, 256), 0)
    b_col = lax.broadcasted_iota(jnp.int32, (256, 256), 1)
    equal = ncol == nrow
    earlier = jnp.where(equal & (b_row < b_col), 1.0, 0.0)
    leads = jnp.sum(earlier, axis=0, keepdims=True) == 0.0
    merge = jnp.where(equal & leads, 1.0, 0.0).astype(BF16)
    at_ends = jnp.where(gid == ends_row, 1.0, 0.0).astype(BF16)
    at_st = jnp.where(gid == st_row, 1.0, 0.0).astype(BF16)
    for i in range(6, 11):
        fetches[i].wait()
    delay = twice_over(delay_ref[...])
    twice = 2.0 * twice_over(admit_ref[...])
    in_service = twice_over(breaker_ref[...].astype(F32))
    flips = twice_over(jnp.where(flip, 1, 0))
    end_of = 2 * jnp.where(low, lane, lane - 64) + jnp.where(low, flips, 1 - flips)
    perm = jnp.where(row == end_of, 1.0, 0.0).astype(BF16)
    hist = jnp.concatenate([hv_ref[t] for t in range(DMAX)] + [hj_ref[t] for t in range(DMAX)], axis=0)
    hist = dot(jnp.concatenate(split3(hist), axis=0).astype(BF16), perm)
    hist = hist[0:48] + hist[48:96] + hist[96:144]
    volts = [hist[4 * t : 4 * t + 4] for t in range(DMAX)]
    injs = [hist[24 + 4 * t : 28 + 4 * t] for t in range(DMAX)]

    await_recv(ex1x)
    parts = [buf1x[p].astype(F32) for p in range(NX)]
    block = parts[0][0:16]
    for part in parts[1:]:
        block += part[0:16]
    wsend[...] = block.astype(BF16)
    exw = []
    for dz in (1, -1, 2, -2, 3, 0):
        for dk in (0, 1):
            if dz or dk:
                k_to = lax.rem(core + dk, 2)
                z_to, z_from = lax.rem(z + dz + 12, 12), lax.rem(z - dz + 12, 12)
                exw.append(
                    ({"col": z_to * 2 + k_to}, lax.rem(z_from, 6) * 2 + k_to, piece, wsend, wbuf, sw, rw)
                )
    push(exw)
    wbuf[piece] = wsend[...]
    for p in range(NY):
        for q in range(NX // 2):
            a = parts[2 * q][16 + 4 * p : 20 + 4 * p]
            b = parts[2 * q + 1][16 + 4 * p : 20 + 4 * p]
            m = (2 * p + q) * 128
            s_ref[0:4, m : m + 128] = jnp.where(low, a, pltpu.roll(b, 64, 1))
            s_ref[4:8, m : m + 128] = jnp.where(low, pltpu.roll(a, 64, 1), b)
    both = lax.dot_general(s_ref[...].astype(BF16), inv_ref[...], NT, preferred_element_type=F32)
    source_part = jnp.where(low, both[0:4], both[4:8])
    send2y[16:20, :] = exact_dot(source_part, at_ends)
    send2y[20:24, :] = exact_dot(source_part, at_st)

    await_recv(ex0)
    t_ref[...] = jnp.zeros((128, 128), F32)
    for p in range(NC):
        t_ref[2 * p : 2 * p + 2, :] = buf0[p]
    stations = t_ref[...].T
    send2y[0:16, :] = jnp.where(low, stations[0:16], pltpu.roll(stations[16:32], 64, 1))
    ex2y = ring(NY, y, to_y, lambda p: send2y, buf2y, s2y, r2y)
    push(ex2y)
    buf2y[y] = send2y[...]

    await_recv(exw)
    w = jnp.concatenate([wbuf[p].astype(F32) for p in range(12)], axis=0)
    high_w = pltpu.roll(w, 64, 1)
    is_high = col192 >= NS
    w_ends = jnp.where(low, jnp.where(is_high, 0.0, w), jnp.where(is_high, high_w, 0.0))
    w_st = jnp.where(low, high_w, 0.0)
    w_full = jnp.concatenate(
        [jnp.concatenate([w_ends, w_st], axis=1), jnp.zeros((64, 256), F32)], axis=0
    ).astype(BF16)

    await_recv(ex2y)
    total = buf2y[0]
    for p in range(1, NY):
        total += buf2y[p]
    send2x[...] = total
    ex2x = ring(NX, x, to_x, lambda p: send2x, buf2x, s2x, r2x)
    push(ex2x)
    buf2x[x] = total

    await_recv(ex2x)
    total = buf2x[0]
    for p in range(1, NX):
        total += buf2x[p]
    sums = jnp.where(
        station_lane,
        jnp.concatenate([total[0:16], pltpu.roll(total[0:16], 64, 1)], axis=0),
        0.0,
    )
    src_nodes = jnp.concatenate([total[16:20], total[20:24]], axis=1)

    counts = [jnp.where(station_lane, stations[32 + 4 * n : 36 + 4 * n], 0.0) for n in range(STEPS)]
    node_volt = jnp.where(station_lane, stations[64:68], 0.0)
    currents = []
    for n in range(STEPS):
        u, j = volts[n + DMAX - DMIN], injs[n + DMAX - DMIN]
        for d in range(DMIN + 1, DMAX + 1):
            u = jnp.where(delay == d, volts[n + DMAX - d], u)
            j = jnp.where(delay == d, injs[n + DMAX - d], j)
        injection = in_service * (twice * pltpu.roll(u, 64, 1) - pltpu.roll(j, 64, 1))
        injs.append(injection)
        charge = sums[4 * n : 4 * n + 4]
        for q in range(n):
            charge -= 0.5 * jnp.minimum(counts[n], counts[q]) * currents[q]
        current = (2.0 / SM * charge - node_volt) / (1.0 + counts[n] / SM)
        current = jnp.where(station_lane, current, 0.0)
        currents.append(current)
        term = exact_dot(jnp.concatenate([injection, current], axis=1), merge)
        term = jnp.concatenate([term, jnp.zeros_like(term)], axis=0).astype(BF16)
        if n + 1 < STEPS:
            nodes = dot(term, w_full)[0:4] + src_nodes
            volts.append(nodes[:, 0:128])
            node_volt = nodes[:, 128:256]

    t_ref[0:32, :] = jnp.concatenate(currents, axis=0)
    t_ref[32:128, :] = jnp.zeros((96, 128), F32)
    out = t_ref[...].T
    for p in range(NC):
        send3[p] = out[2 * p : 2 * p + 2, :]
    ex3 = ring(NC, col, to_c, lambda p: send3.at[p], buf3, s3, r3)
    push(ex3)
    buf3[col] = send3[col]
    last = dot(term, jnp.concatenate([gt, jnp.zeros((64, 128), F32)], axis=0).astype(BF16))
    final = source_part + last[0:4]
    for c in range(4):
        volt_ref[c] = jnp.concatenate([final[c : c + 1, 0:64], final[c : c + 1, 64:128]], axis=0)
    spread = [jnp.where(row == 4 * n + lax.rem(lane, 4), 1.0, 0.0).astype(BF16) for n in range(STEPS)]
    spread = jnp.concatenate(spread, axis=1)
    for ex in (ex0, ex1y, ex1x, exw, ex2y, ex2x):
        await_send(ex)
    await_recv(ex3)
    for p in range(NC):
        t_ref[2 * p : 2 * p + 2, :] = buf3[p]
    wide = dot(jnp.concatenate(split3(t_ref[0:48, :]), axis=0).astype(BF16), spread)
    wide = wide[0:48] + wide[48:96] + wide[96:144]
    discharge = jnp.zeros((75, 2, 96), F32)
    for n in range(STEPS):
        tile = jnp.where(owner, wide[:, 128 * n : 128 * n + 128], 0.0)
        rows = [jnp.sum(jnp.where(second == s, tile, 0.0), axis=0, keepdims=True) for s in (False, True)]
        current = jnp.concatenate(rows, axis=0)[:, 0:96]
        cur_out[n] = current
        discharge += jnp.where(position < count_ref[n][None], current[None], 0.0)
    cap_out[...] = cap_ref[...] - 0.5 * discharge
    await_send(ex3)


def write_kernel(a, b, c, x, y, z, sems):
    copies = [pltpu.make_async_copy(s, d, sems.at[i]) for i, (s, d) in enumerate(((a, x), (b, y), (c, z)))]
    for copy in copies:
        copy.start()
    for copy in copies:
        copy.wait()


def exchange(*inputs):
    vmem, hbm = pl.BlockSpec(memory_space=pltpu.VMEM), pl.BlockSpec(memory_space=HBM)
    pairs = lambda n: [pltpu.SemaphoreType.DMA((n,)), pltpu.SemaphoreType.DMA((n,))]
    outs = tuple(jax.ShapeDtypeStruct(s, F32) for s in ((4, 2, 64), (75, 2, 96), (STEPS, 2, 96)))
    fetched = [inputs[0]] + list(inputs[2:])
    results = pl.pallas_call(
        kernel,
        out_shape=outs,
        in_specs=[hbm, vmem] + [hbm] * 10,
        out_specs=(vmem,) * 3,
        scratch_shapes=[
            *(pltpu.VMEM(v.shape, v.dtype) for v in fetched),
            pltpu.VMEM((192, 128), F32),
            pltpu.VMEM((8, NS), F32),
            pltpu.VMEM((128, 128), F32),
            pltpu.VMEM((40, 128), F32),
            pltpu.VMEM((32, 128), BF16),
            pltpu.VMEM((NY, 32, 128), BF16),
            pltpu.VMEM((48, 128), BF16),
            pltpu.VMEM((NX, 48, 128), BF16),
            pltpu.VMEM((16, 128), BF16),
            pltpu.VMEM((12, 16, 128), BF16),
            pltpu.VMEM((NC, 2, 128), F32),
            pltpu.VMEM((NC, 2, 128), F32),
            pltpu.VMEM((24, 128), F32),
            pltpu.VMEM((NY, 24, 128), F32),
            pltpu.VMEM((24, 128), F32),
            pltpu.VMEM((NX, 24, 128), F32),
            pltpu.VMEM((NC, 2, 128), F32),
            pltpu.VMEM((NC, 2, 128), F32),
            pltpu.SemaphoreType.DMA((11,)),
            *pairs(NC), *pairs(NY), *pairs(NX), *pairs(12), *pairs(NY), *pairs(NX), *pairs(NC),
        ],
        compiler_params=pltpu.CompilerParams(
            collective_id=0, has_side_effects=True, vmem_limit_bytes=60 * 1024 * 1024
        ),
    )(*inputs)
    return pl.pallas_call(
        write_kernel,
        out_shape=outs,
        in_specs=[vmem] * 3,
        out_specs=(hbm,) * 3,
        scratch_shapes=[pltpu.SemaphoreType.DMA((3,))],
        compiler_params=pltpu.CompilerParams(vmem_limit_bytes=60 * 1024 * 1024),
    )(*results)


def per_device(
    inv_conductance, source, line_ends, delays, admittance, breaker, hist_volt, hist_inj,
    station_node, station_initial, capacitor_initial, insert_count,
):
    volts, capacitor, current = exchange(
        inv_conductance.reshape(128, NS), source, line_ends.T, delays[None, :], admittance[None, :],
        breaker.T, hist_volt, hist_inj, station_node[None, :], station_initial.T,
        capacitor_initial.transpose(2, 1, 0), insert_count.transpose(0, 2, 1),
    )
    return volts, capacitor.transpose(2, 1, 0), current.transpose(0, 2, 1)


def solution(mesh):
    in_specs = (
        P(None, "sub", None),
        P("col", None, "sub"),
        P(),
        P(),
        P(),
        P(None, "col"),
        P(None, "col", None),
        P(None, "col", None),
        P(),
        P(None, "col"),
        P(None, "col", "sub"),
        P(None, None, "col"),
    )
    out_specs = (P("col", None, "sub"), P(None, "col", "sub"), P(None, None, "col"))
    return jax.shard_map(
        per_device, mesh=mesh, in_specs=in_specs, out_specs=out_specs, check_vma=False
    )
```

time: 59.9 us -> 51.3 us (0.86)
  local copies, waits for them, and re-layouts: 10.6 us -> 0 us
  Pallas kernels: 47.1 us -> 50.5 us
  other arithmetic: 0.92 us -> 0 us
    unnamed x32 -> x0, local copies, waits for them, and re-layouts: 8.32 us -> none
    pallas_call x1 -> x2, Pallas kernels: 47.1 us -> 50.5 us  [the longest x1 48.9 us: exchange(): pl.pallas_call(kernel, out_shape=outs, in_specs=[hbm, vmem] + [hbm] * 10,...]
    reshape x6 -> x0, local copies, waits for them, and re-layouts: 1.04 us -> none  [the longest x1 0.67 us: per_device(): return (volts.reshape(4, 2, 64), capacitor, current)]
where the time goes in v2:
time: 51.3 us; the launch traced here: 51.1 us
  Pallas kernels  50.5 us (98%)
  between operations  0.64 us (1%)
    pallas_call x1, Pallas kernels, exchange(): pl.pallas_call(kernel, out_shape=outs, in_specs=[hbm, vmem] + [hbm] * 10,...  48.9 us
    pallas_call x1, Pallas kernels, exchange(): pl.pallas_call(write_kernel, out_shape=outs, in_specs=[vmem] * 3, out_spe...  1.55 us

profile of v2, /device:TPU:1, one launch (start us, length us, event | category | flops | bytes accessed | tf_op | source)
XLA Modules:
  0.0 51.1 jit_solution(4324815451389933894)
XLA Ops:
  0.6 48.9 %shard_map.139 = (f32[4,2,64]{2,1,0:T(2,128)}, f32[75,2,96]{2,1,0:T(2,128)}, f32[8,2,96]{2,1,0:T(2,128)}) custom-call(bf16[128,2048]{1,0:T(8,128)(2,1)} %bitcast.11, bf16[4,2,64]{2,1,0:T(2,128)(2,1)} %src_in.1, s32[2,64]{1,0:T(2,128)} %bitcast.15, s32[1,64]{1,0:T(1,128)} %bitcast.17, f32[1,64]{1,0:T(1,128)} %bitcast.18, s32[4,64]{1,0:T(4,128)} %bitcast.14, ...), custom_call_target="tpu_custom_call" | custom-call | tf_op jit(solution)/shard_map/pallas_call | solution.py:344
  49.6 1.6 %shard_map.140 = (f32[4,2,64]{2,1,0:T(2,128)}, f32[75,2,96]{2,1,0:T(2,128)}, f32[8,2,96]{2,1,0:T(2,128)}) custom-call(f32[4,2,64]{2,1,0:T(2,128)} %get-tuple-element.9.a, f32[75,2,96]{2,1,0:T(2,128)} %get-tuple-element.10.b, f32[8,2,96]{2,1,0:T(2,128)} %get-tuple-element.11.c), custom_call_target="tpu_custom_call" | custom-call | tf_op jit(solution)/shard_map/pallas_call | solution.py:376

commit v3 on v2

--- a/solution.py
+++ b/solution.py
@@ -38,8 +38,8 @@
     inv_hbm, src_in, ends_hbm, delay_hbm, admit_hbm, breaker_hbm, hv_hbm, hj_hbm, node_hbm, init_hbm, cap_hbm, count_hbm,
     volt_ref, cap_out, cur_out,
     inv_ref, ends_ref, delay_ref, admit_ref, breaker_ref, hv_ref, hj_ref, node_ref, init_ref, cap_ref, count_ref,
-    gt_ref, s_ref, t_ref, q_ref, send1y, buf1y, send1x, buf1x, wsend, wbuf, msg0, buf0, send2y, buf2y, send2x, buf2x, send3, buf3,
-    loads, s0, r0, s1y, r1y, s1x, r1x, sw, rw, s2y, r2y, s2x, r2x, s3, r3,
+    gt_ref, s_ref, t_ref, q_ref, sends, bufs, send1y, buf1y, send1x, buf1x, wsend, wbuf, msg0, buf0, send2y, buf2y, send2x, buf2x, send3, buf3,
+    loads, s0, r0, ss, rs, s1y, r1y, s1x, r1x, sw, rw, s2y, r2y, s2x, r2x, s3, r3,
 ):
     sub, col = lax.axis_index("sub"), lax.axis_index("col")
     y, x = sub // NX, lax.rem(sub, NX)
@@ -48,10 +48,18 @@
     to_x = lambda p: {"sub": y * NX + p}
     to_c = lambda p: {"col": p}
 
+    far = lambda n: sorted(range(1, n), key=lambda d: -min(d, n - d))
+
     def ring(n, me, to, src, dst, send, recv):
-        return [
-            (to(p), p, me, src(p), dst, send, recv) for p in [lax.rem(me + d, n) for d in range(1, n)]
-        ]
+        return [(to(p), p, me, src(p), dst, send, recv) for p in [lax.rem(me + d, n) for d in far(n)]]
+
+    def plane(src, dst, send, recv):
+        offsets = sorted(
+            [(dy, dx) for dy in range(NY) for dx in range(NX) if dy or dx],
+            key=lambda o: -(min(o[0], NY - o[0]) + min(o[1], NX - o[1])),
+        )
+        peers = [lax.rem(y + dy, NY) * NX + lax.rem(x + dx, NX) for dy, dx in offsets]
+        return [({"sub": p}, p, sub, src, dst, send, recv) for p in peers]
 
     def copies(exchange):
         return [
@@ -90,57 +98,16 @@
     for fetch in fetches:
         fetch.start()
     barrier = pltpu.get_barrier_semaphore()
-    for n, me, to in ((NY, y, to_y), (NX, x, to_x), (NC, col, to_c)):
-        for d in range(1, n):
-            pl.semaphore_signal(
-                barrier, inc=1, device_id=to(lax.rem(me + d, n)), device_id_type=MESH
-            )
+    greeted = [to_c(lax.rem(col + d, NC)) for d in far(NC)]
+    greeted += [peer[0] for peer in plane(None, None, None, None)]
+    for device in greeted:
+        pl.semaphore_signal(barrier, inc=1, device_id=device, device_id_type=MESH)
 
     lane = lax.broadcasted_iota(jnp.int32, (1, 128), 1)
     row = lax.broadcasted_iota(jnp.int32, (128, 1), 0)
     low = lane < 64
     station_lane = lane < 48
     twice_over = lambda v: jnp.concatenate([v, v], axis=1)
-
-    fetches[0].wait()
-    fetches[1].wait()
-    e0, e1 = ends_ref[0:1, :], ends_ref[1:2, :]
-    flip = e0 >= NS
-    ends_row = jnp.concatenate([jnp.where(flip, e1, e0), jnp.where(flip, e0, e1)], axis=1)
-    st_row = jnp.concatenate([node_ref[...], jnp.zeros((1, 80), jnp.int32)], axis=1)
-    st_row = jnp.where(station_lane, st_row, -1 - lane)
-    ends_col = jnp.broadcast_to(ends_row, (128, 128)).T
-    st_col = jnp.broadcast_to(st_row, (128, 128)).T
-    col192 = jnp.concatenate([ends_col, st_col[0:64]], axis=0)
-
-    place = lax.rem(col192, NS)
-    fetches[2].wait()
-    acc = jnp.zeros((192, 128), F32)
-    for k in range(0, NS, 256):
-        halves = [jnp.where(place == lane + (k + h), 1.0, 0.0).astype(BF16) for h in (0, 128)]
-        acc += lax.dot_general(
-            jnp.concatenate(halves, axis=1), inv_ref[:, k : k + 256], NT, preferred_element_type=F32
-        )
-    gt = jnp.where((col192 >= NS) == jnp.broadcast_to(lane >= 64, (192, 128)), acc, 0.0)
-    gt_ref[...] = gt
-
-    gid = jnp.where(row >= 64, NS - 64, 0) + row + sub * 64
-    st_high = pltpu.roll(st_row, 64, 1)
-    row0 = jnp.where(low, ends_row, st_high)
-    row1 = jnp.where(low, pltpu.roll(ends_row, 64, 1), st_high)
-    pick = jnp.where(gid == jnp.where(row >= 64, row1, row0), 1.0, 0.0).astype(BF16)
-    piece = lax.rem(z, 6) * 2 + core
-    mine = gt_ref[pl.ds(pl.multiple_of(piece * 16, 16), 16), :]
-    for c in range(4):
-        pair = src_in[c].astype(F32)
-        s_ref[c : c + 1, 0:128] = jnp.concatenate([pair[0:1], pair[1:2]], axis=1)
-    first_part = [dot(mine.astype(BF16), pick), s_ref[0:4, 0:128], jnp.zeros((12, 128), F32)]
-    send1y[...] = jnp.concatenate(first_part, axis=0).astype(BF16)
-    pl.semaphore_wait(barrier, NC + NY + NX - 3)
-
-    ex1y = ring(NY, y, to_y, lambda p: send1y, buf1y, s1y, r1y)
-    push(ex1y)
-    buf1y[y] = send1y[...]
 
     for i in (3, 4, 5):
         fetches[i].wait()
@@ -166,19 +133,52 @@
     moved = moved[0:48] + moved[48:96] + moved[96:144]
     for p in range(NC):
         msg0[p] = moved[2 * p : 2 * p + 2]
+    for c in range(4):
+        pair = src_in[c].astype(F32)
+        sends[c : c + 1, :] = jnp.concatenate([pair[0:1], pair[1:2]], axis=1)
+    pl.semaphore_wait(barrier, NC + NX * NY - 2)
     ex0 = ring(NC, col, to_c, lambda p: msg0.at[p], buf0, s0, r0)
     push(ex0)
     buf0[col] = msg0[col]
 
-    await_recv(ex1y)
-    parts = [buf1y[p].astype(F32) for p in range(NY)]
-    total = parts[0][0:16]
-    for part in parts[1:]:
-        total += part[0:16]
-    send1x[...] = jnp.concatenate([total] + [part[16:20] for part in parts], axis=0).astype(BF16)
-    ex1x = ring(NX, x, to_x, lambda p: send1x, buf1x, s1x, r1x)
-    push(ex1x)
-    buf1x[x] = send1x[...]
+    exs = plane(sends, bufs, ss, rs)
+    push(exs)
+    bufs[sub] = sends[...]
+
+    fetches[0].wait()
+    fetches[1].wait()
+    e0, e1 = ends_ref[0:1, :], ends_ref[1:2, :]
+    flip = e0 >= NS
+    ends_row = jnp.concatenate([jnp.where(flip, e1, e0), jnp.where(flip, e0, e1)], axis=1)
+    st_row = jnp.concatenate([node_ref[...], jnp.zeros((1, 80), jnp.int32)], axis=1)
+    st_row = jnp.where(station_lane, st_row, -1 - lane)
+    ends_col = jnp.broadcast_to(ends_row, (128, 128)).T
+    st_col = jnp.broadcast_to(st_row, (128, 128)).T
+    col192 = jnp.concatenate([ends_col, st_col[0:64]], axis=0)
+
+    place = lax.rem(col192, NS)
+    fetches[2].wait()
+    acc = jnp.zeros((192, 128), F32)
+    for k in range(0, NS, 256):
+        halves = [jnp.where(place == lane + (k + h), 1.0, 0.0).astype(BF16) for h in (0, 128)]
+        acc += lax.dot_general(
+            jnp.concatenate(halves, axis=1), inv_ref[:, k : k + 256], NT, preferred_element_type=F32
+        )
+    gt = jnp.where((col192 >= NS) == jnp.broadcast_to(lane >= 64, (192, 128)), acc, 0.0)
+    gt_ref[...] = gt
+
+    gid = jnp.where(row >= 64, NS - 64, 0) + row + sub * 64
+    st_high = pltpu.roll(st_row, 64, 1)
+    row0 = jnp.where(low, ends_row, st_high)
+    row1 = jnp.where(low, pltpu.roll(ends_row, 64, 1), st_high)
+    pick = jnp.where(gid == jnp.where(row >= 64, row1, row0), 1.0, 0.0).astype(BF16)
+    piece = lax.rem(z, 6) * 2 + core
+    mine = gt_ref[pl.ds(pl.multiple_of(piece * 16, 16), 16), :]
+    send1y[...] = dot(mine.astype(BF16), pick).astype(BF16)
+
+    ex1y = ring(NY, y, to_y, lambda p: send1y, buf1y, s1y, r1y)
+    push(ex1y)
+    buf1y[y] = send1y[...]
 
     nrow = jnp.concatenate([ends_row, st_row], axis=1)
     ncol = jnp.concatenate([twice_over(ends_col), twice_over(st_col)], axis=0)
@@ -204,11 +204,44 @@
     volts = [hist[4 * t : 4 * t + 4] for t in range(DMAX)]
     injs = [hist[24 + 4 * t : 28 + 4 * t] for t in range(DMAX)]
 
+    await_recv(exs)
+    for p in range(NY):
+        for q in range(NX // 2):
+            a = bufs[4 * p + 2 * q]
+            b = bufs[4 * p + 2 * q + 1]
+            m = (2 * p + q) * 128
+            s_ref[0:4, m : m + 128] = jnp.where(low, a, pltpu.roll(b, 64, 1))
+            s_ref[4:8, m : m + 128] = jnp.where(low, pltpu.roll(a, 64, 1), b)
+    both = lax.dot_general(s_ref[...].astype(BF16), inv_ref[...], NT, preferred_element_type=F32)
+    source_part = jnp.where(low, both[0:4], both[4:8])
+    send2y[16:20, :] = exact_dot(source_part, at_ends)
+    send2y[20:24, :] = exact_dot(source_part, at_st)
+
+    await_recv(ex0)
+    t_ref[...] = jnp.zeros((128, 128), F32)
+    for p in range(NC):
+        t_ref[2 * p : 2 * p + 2, :] = buf0[p]
+    stations = t_ref[...].T
+    send2y[0:16, :] = jnp.where(low, stations[0:16], pltpu.roll(stations[16:32], 64, 1))
+    ex2y = ring(NY, y, to_y, lambda p: send2y, buf2y, s2y, r2y)
+    push(ex2y)
+    buf2y[y] = send2y[...]
+
+    await_recv(ex1y)
+    parts = [buf1y[p].astype(F32) for p in range(NY)]
+    total = parts[0]
+    for part in parts[1:]:
+        total += part
+    send1x[...] = total.astype(BF16)
+    ex1x = ring(NX, x, to_x, lambda p: send1x, buf1x, s1x, r1x)
+    push(ex1x)
+    buf1x[x] = send1x[...]
+
     await_recv(ex1x)
     parts = [buf1x[p].astype(F32) for p in range(NX)]
-    block = parts[0][0:16]
+    block = parts[0]
     for part in parts[1:]:
-        block += part[0:16]
+        block += part
     wsend[...] = block.astype(BF16)
     exw = []
     for dz in (1, -1, 2, -2, 3, 0):
@@ -221,27 +254,15 @@
                 )
     push(exw)
     wbuf[piece] = wsend[...]
-    for p in range(NY):
-        for q in range(NX // 2):
-            a = parts[2 * q][16 + 4 * p : 20 + 4 * p]
-            b = parts[2 * q + 1][16 + 4 * p : 20 + 4 * p]
-            m = (2 * p + q) * 128
-            s_ref[0:4, m : m + 128] = jnp.where(low, a, pltpu.roll(b, 64, 1))
-            s_ref[4:8, m : m + 128] = jnp.where(low, pltpu.roll(a, 64, 1), b)
-    both = lax.dot_general(s_ref[...].astype(BF16), inv_ref[...], NT, preferred_element_type=F32)
-    source_part = jnp.where(low, both[0:4], both[4:8])
-    send2y[16:20, :] = exact_dot(source_part, at_ends)
-    send2y[20:24, :] = exact_dot(source_part, at_st)
-
-    await_recv(ex0)
-    t_ref[...] = jnp.zeros((128, 128), F32)
-    for p in range(NC):
-        t_ref[2 * p : 2 * p + 2, :] = buf0[p]
-    stations = t_ref[...].T
-    send2y[0:16, :] = jnp.where(low, stations[0:16], pltpu.roll(stations[16:32], 64, 1))
-    ex2y = ring(NY, y, to_y, lambda p: send2y, buf2y, s2y, r2y)
-    push(ex2y)
-    buf2y[y] = send2y[...]
+
+    await_recv(ex2y)
+    total = buf2y[0]
+    for p in range(1, NY):
+        total += buf2y[p]
+    send2x[...] = total
+    ex2x = ring(NX, x, to_x, lambda p: send2x, buf2x, s2x, r2x)
+    push(ex2x)
+    buf2x[x] = total
 
     await_recv(exw)
     w = jnp.concatenate([wbuf[p].astype(F32) for p in range(12)], axis=0)
@@ -252,15 +273,6 @@
     w_full = jnp.concatenate(
         [jnp.concatenate([w_ends, w_st], axis=1), jnp.zeros((64, 256), F32)], axis=0
     ).astype(BF16)
-
-    await_recv(ex2y)
-    total = buf2y[0]
-    for p in range(1, NY):
-        total += buf2y[p]
-    send2x[...] = total
-    ex2x = ring(NX, x, to_x, lambda p: send2x, buf2x, s2x, r2x)
-    push(ex2x)
-    buf2x[x] = total
 
     await_recv(ex2x)
     total = buf2x[0]
@@ -310,7 +322,7 @@
         volt_ref[c] = jnp.concatenate([final[c : c + 1, 0:64], final[c : c + 1, 64:128]], axis=0)
     spread = [jnp.where(row == 4 * n + lax.rem(lane, 4), 1.0, 0.0).astype(BF16) for n in range(STEPS)]
     spread = jnp.concatenate(spread, axis=1)
-    for ex in (ex0, ex1y, ex1x, exw, ex2y, ex2x):
+    for ex in (ex0, exs, ex1y, ex1x, exw, ex2y, ex2x):
         await_send(ex)
     await_recv(ex3)
     for p in range(NC):
@@ -352,10 +364,12 @@
             pltpu.VMEM((8, NS), F32),
             pltpu.VMEM((128, 128), F32),
             pltpu.VMEM((40, 128), F32),
-            pltpu.VMEM((32, 128), BF16),
-            pltpu.VMEM((NY, 32, 128), BF16),
-            pltpu.VMEM((48, 128), BF16),
-            pltpu.VMEM((NX, 48, 128), BF16),
+            pltpu.VMEM((4, 128), F32),
+            pltpu.VMEM((NX * NY, 4, 128), F32),
+            pltpu.VMEM((16, 128), BF16),
+            pltpu.VMEM((NY, 16, 128), BF16),
+            pltpu.VMEM((16, 128), BF16),
+            pltpu.VMEM((NX, 16, 128), BF16),
             pltpu.VMEM((16, 128), BF16),
             pltpu.VMEM((12, 16, 128), BF16),
             pltpu.VMEM((NC, 2, 128), F32),
@@ -367,7 +381,7 @@
             pltpu.VMEM((NC, 2, 128), F32),
             pltpu.VMEM((NC, 2, 128), F32),
             pltpu.SemaphoreType.DMA((11,)),
-            *pairs(NC), *pairs(NY), *pairs(NX), *pairs(12), *pairs(NY), *pairs(NX), *pairs(NC),
+            *pairs(NC), *pairs(NX * NY), *pairs(NY), *pairs(NX), *pairs(12), *pairs(NY), *pairs(NX), *pairs(NC),
         ],
         compiler_params=pltpu.CompilerParams(
             collective_id=0, has_side_effects=True, vmem_limit_bytes=60 * 1024 * 1024

time: 51.3 us -> 49.3 us (0.961)
  Pallas kernels: 50.5 us -> 48.4 us
    pallas_call x1, Pallas kernels: 48.9 us -> 46.9 us  [exchange(): pl.pallas_call(kernel, out_shape=outs, in_specs=[hbm, vmem] + [hbm] * 10,...]
where the time goes in v3:
time: 49.3 us; the launch traced here: 49.1 us
  Pallas kernels  48.4 us (98%)
  between operations  0.64 us (1%)
    pallas_call x1, Pallas kernels, exchange(): pl.pallas_call(kernel, out_shape=outs, in_specs=[hbm, vmem] + [hbm] * 10,...  46.9 us
    pallas_call x1, Pallas kernels, exchange(): pl.pallas_call(write_kernel, out_shape=outs, in_specs=[vmem] * 3, out_spe...  1.55 us

profile of v3, /device:TPU:1, one launch (start us, length us, event | category | flops | bytes accessed | tf_op | source)
XLA Modules:
  0.0 49.1 jit_solution(2069288669664702106)
XLA Ops:
  0.6 46.9 %shard_map.139 = (f32[4,2,64]{2,1,0:T(2,128)}, f32[75,2,96]{2,1,0:T(2,128)}, f32[8,2,96]{2,1,0:T(2,128)}) custom-call(bf16[128,2048]{1,0:T(8,128)(2,1)} %bitcast.11, bf16[4,2,64]{2,1,0:T(2,128)(2,1)} %src_in.1, s32[2,64]{1,0:T(2,128)} %bitcast.15, s32[1,64]{1,0:T(1,128)} %bitcast.17, f32[1,64]{1,0:T(1,128)} %bitcast.18, s32[4,64]{1,0:T(4,128)} %bitcast.14, ...), custom_call_target="tpu_custom_call" | custom-call | tf_op jit(solution)/shard_map/pallas_call | solution.py:356
  47.5 1.6 %shard_map.140 = (f32[4,2,64]{2,1,0:T(2,128)}, f32[75,2,96]{2,1,0:T(2,128)}, f32[8,2,96]{2,1,0:T(2,128)}) custom-call(f32[4,2,64]{2,1,0:T(2,128)} %get-tuple-element.9.a, f32[75,2,96]{2,1,0:T(2,128)} %get-tuple-element.10.b, f32[8,2,96]{2,1,0:T(2,128)} %get-tuple-element.11.c), custom_call_target="tpu_custom_call" | custom-call | tf_op jit(solution)/shard_map/pallas_call | solution.py:390

commit v4 on v3

--- a/solution.py
+++ b/solution.py
@@ -341,7 +341,8 @@
 
 
 def write_kernel(a, b, c, x, y, z, sems):
-    copies = [pltpu.make_async_copy(s, d, sems.at[i]) for i, (s, d) in enumerate(((a, x), (b, y), (c, z)))]
+    pieces = [(a, x), (c, z)] + [(b.at[pl.ds(k, 15)], y.at[pl.ds(k, 15)]) for k in range(0, 75, 15)]
+    copies = [pltpu.make_async_copy(s, d, sems.at[i]) for i, (s, d) in enumerate(pieces)]
     for copy in copies:
         copy.start()
     for copy in copies:
@@ -392,7 +393,7 @@
         out_shape=outs,
         in_specs=[vmem] * 3,
         out_specs=(hbm,) * 3,
-        scratch_shapes=[pltpu.SemaphoreType.DMA((3,))],
+        scratch_shapes=[pltpu.SemaphoreType.DMA((7,))],
         compiler_params=pltpu.CompilerParams(vmem_limit_bytes=60 * 1024 * 1024),
     )(*results)
 

time: 49.3 us -> 49.3 us (level)
  no operation moved by 1% of the time
where the time goes in v4:
time: 49.3 us; the launch traced here: 49.1 us
  Pallas kernels  48.5 us (98%)
  between operations  0.64 us (1%)
    pallas_call x1, Pallas kernels, exchange(): pl.pallas_call(kernel, out_shape=outs, in_specs=[hbm, vmem] + [hbm] * 10,...  46.9 us
    pallas_call x1, Pallas kernels, exchange(): pl.pallas_call(write_kernel, out_shape=outs, in_specs=[vmem] * 3, out_spe...  1.58 us

profile of v4, /device:TPU:1, one launch (start us, length us, event | category | flops | bytes accessed | tf_op | source)
XLA Modules:
  0.0 49.1 jit_solution(14914802028461897706)
XLA Ops:
  0.6 46.9 %shard_map.139 = (f32[4,2,64]{2,1,0:T(2,128)}, f32[75,2,96]{2,1,0:T(2,128)}, f32[8,2,96]{2,1,0:T(2,128)}) custom-call(bf16[128,2048]{1,0:T(8,128)(2,1)} %bitcast.11, bf16[4,2,64]{2,1,0:T(2,128)(2,1)} %src_in.1, s32[2,64]{1,0:T(2,128)} %bitcast.15, s32[1,64]{1,0:T(1,128)} %bitcast.17, f32[1,64]{1,0:T(1,128)} %bitcast.18, s32[4,64]{1,0:T(4,128)} %bitcast.14, ...), custom_call_target="tpu_custom_call" | custom-call | tf_op jit(solution)/shard_map/pallas_call | solution.py:357
  47.5 1.6 %shard_map.140 = (f32[4,2,64]{2,1,0:T(2,128)}, f32[75,2,96]{2,1,0:T(2,128)}, f32[8,2,96]{2,1,0:T(2,128)}) custom-call(f32[4,2,64]{2,1,0:T(2,128)} %get-tuple-element.9.a, f32[75,2,96]{2,1,0:T(2,128)} %get-tuple-element.10.b, f32[8,2,96]{2,1,0:T(2,128)} %get-tuple-element.11.c), custom_call_target="tpu_custom_call" | custom-call | tf_op jit(solution)/shard_map/pallas_call | solution.py:391
